TPU v7x, 128 devices: a whole 4x4x4 slice. The times are simulated.
128 devices in a mesh: tm: 32 (over z, y, x_lo), slab: 4 (over x_hi, core).
Axes of the slice: x: 4 (x_hi: 2, x_lo: 2; x = x_hi * 2 + x_lo), y: 4, z: 4, core: 2. Of those that a mesh axis runs over, the one named last changes fastest.
Arguments:
- kspace: bfloat16 [2, 64, 4, 96, 9984], P(None, 'tm', None, 'slab'), may hold values from -40 to 40, as said below
- sens: float32 [2, 4, 8, 104, 96], P(None, None, None, 'slab'), may hold values from -3 to 3
Outputs:
- projected: float32 [64, 2, 8, 104, 96], P('tm', None, None, 'slab')
Inputs may be any that keep to these rules, and one draw needn't show every extreme that they name: `kspace`: k-space values of order one with frames of different scale.
All inputs are finite; a program needn't handle non-finite values.
Results may differ from a plain program's by a relative error of at most 0.0036.
Values may be sent and summed in bfloat16 or wider, within the bound.
A program may use at most 128 MiB of HBM per device.

v0:
```python
import jax
import jax.numpy as jnp
from jax import lax
from jax.sharding import PartitionSpec as P

NX = 96
NY = 104
NZ = 96
RANK = 32
ITERS = 4
XW = 8


def shifted(shard, axis, by):
    size = lax.axis_size(axis)
    pairs = [(i, i + by) for i in range(size) if 0 <= i + by < size]
    return lax.ppermute(shard, axis, pairs)


def broadcast(value, axis, source):
    kept = jnp.where(lax.axis_index(axis) == source, value, 0).astype(value.dtype)
    return lax.psum(kept, axis)


def inverse_table(length, count, offset):
    outputs = jnp.arange(count, dtype=jnp.int32) + offset
    inputs = jnp.arange(length, dtype=jnp.int32)
    phase = outputs[:, None] * inputs[None, :] % length
    angle = phase.astype(jnp.float32) * (2.0 * jnp.pi / length)
    norm_factor = 1.0 / jnp.sqrt(jnp.float32(length))
    return (jnp.cos(angle) * norm_factor, jnp.sin(angle) * norm_factor)


def contract(pattern, matrix_table, operand):
    return jnp.einsum(pattern, matrix_table, operand, precision=lax.Precision.HIGHEST)


def matmul(left, right):
    return jnp.dot(left, right, precision=lax.Precision.HIGHEST)


def orthonormal(rows):
    gram = lax.psum(matmul(rows, rows.T), "slab")
    factor = jnp.linalg.cholesky(gram)
    return lax.linalg.triangular_solve(factor, rows, left_side=True, lower=True)


def project_onto(qrows, stacked):
    return lax.psum(matmul(qrows, stacked.T), "slab")


def truncate(lower_rows, upper_rows):
    stacked = jnp.concatenate([lower_rows, upper_rows], axis=0)
    current = lower_rows + upper_rows
    for sweep_index in range(ITERS):
        qrows = orthonormal(current)
        current = matmul(project_onto(qrows, stacked), stacked)
    qrows = orthonormal(current)
    correlation = project_onto(qrows, stacked)
    coupling = jnp.linalg.cholesky(matmul(correlation, correlation.T))
    return matmul(coupling.T, qrows)


def merge_pair(lower_rows, upper_rows):
    if 2 * lower_rows.shape[0] <= RANK:
        return jnp.concatenate([lower_rows, upper_rows], axis=0)
    return truncate(lower_rows, upper_rows)


def local(kspace, sens):
    frames_dev = kspace.shape[1]
    coil_count = kspace.shape[2]
    depth_dev = kspace.shape[3]
    spectrum = kspace.astype(jnp.float32).reshape(2, frames_dev, coil_count, depth_dev, NX, NY)
    across_cos, across_sin = inverse_table(NX, XW, (NX - XW) // 2)
    down_cos, down_sin = inverse_table(NY, NY, 0)
    depth_cos, depth_sin = inverse_table(NZ, NZ, 0)
    across_real = contract("jx,fczxy->fczjy", across_cos, spectrum[0]) - contract(
        "jx,fczxy->fczjy", across_sin, spectrum[1]
    )
    across_other = contract("jx,fczxy->fczjy", across_cos, spectrum[1]) + contract(
        "jx,fczxy->fczjy", across_sin, spectrum[0]
    )
    down_real = contract("my,fczjy->fczjm", down_cos, across_real) - contract(
        "my,fczjy->fczjm", down_sin, across_other
    )
    down_other = contract("my,fczjy->fczjm", down_cos, across_other) + contract(
        "my,fczjy->fczjm", down_sin, across_real
    )
    planes = jnp.stack([down_real, down_other]).astype(jnp.bfloat16)
    arrived = lax.all_to_all(planes, "slab", split_axis=5, concat_axis=3, tiled=True).astype(
        jnp.float32
    )
    depth_real = contract("wz,fczxy->fcxyw", depth_cos, arrived[0]) - contract(
        "wz,fczxy->fcxyw", depth_sin, arrived[1]
    )
    depth_other = contract("wz,fczxy->fcxyw", depth_cos, arrived[1]) + contract(
        "wz,fczxy->fcxyw", depth_sin, arrived[0]
    )
    sens_real = sens[0][None]
    sens_other = sens[1][None]
    combined_real = jnp.sum(sens_real * depth_real + sens_other * depth_other, axis=1)
    combined_other = jnp.sum(sens_real * depth_other - sens_other * depth_real, axis=1)
    matrix = jnp.stack([combined_real, combined_other], axis=1).reshape(frames_dev, -1)
    group_count = lax.axis_size("tm")
    levels = group_count.bit_length() - 1
    node_basis = matrix
    for tier_index in range(levels):
        partner = shifted(node_basis, "tm", -(2**tier_index))
        node_basis = merge_pair(node_basis, partner)
    node_basis = broadcast(node_basis, "tm", 0)
    root_rows = orthonormal(node_basis)
    loadings = lax.psum(matmul(root_rows, matrix.T), "slab")
    projected = matmul(loadings.T, root_rows)
    return projected.reshape(frames_dev, 2, XW, -1, NZ)


def solution(mesh):
    in_specs = (P(None, "tm", None, "slab", None), P(None, None, None, "slab", None))
    out_specs = P("tm", None, None, "slab", None)
    return jax.shard_map(local, mesh=mesh, in_specs=in_specs, out_specs=out_specs, check_vma=False)
```

profile of v0, /device:TPU:0, one launch (start us, length us, event | category | flops | bytes accessed | tf_op | source)
XLA Modules:
  0.0 1119.2 jit_solution(8216012897883445169)
XLA Ops:
  6.5 5.4 fusion.192
  12.0 13.7 %squeeze.16 = bf16[2,4,24,96,104]{4,3,2,1,0:T(8,128)(2,1)} reshape(bf16[1,2,4,24,9984]{4,3,2,1,0:T(8,128)(2,1)} %get-tuple-element.9) | data formatting | bytes 7667712 | tf_op jit(solution)/shard_map/squeeze | solution.py:78
  25.7 13.8 %squeeze.17 = bf16[2,4,24,96,104]{4,3,2,1,0:T(8,128)(2,1)} reshape(bf16[1,2,4,24,9984]{4,3,2,1,0:T(8,128)(2,1)} %get-tuple-element.10) | data formatting | bytes 7667712 | tf_op jit(solution)/shard_map/squeeze | solution.py:79
  55.1 5.8 copy.55
  60.9 5.0 reshape.60
  65.9 4.4 all-to-all-start
  73.3 8.7 all-to-all-done
  82.0 5.8 reshape.61
  87.8 4.4 copy.107
  105.6 9.7 collective-permute-done
  117.2 15.2 %collective-permute-done.1 = f32[4,39936]{1,0:T(4,128)S(1)} collective-permute-done((f32[4,39936]{1,0:T(4,128)S(1)}, f32[4,39936]{1,0:T(4,128)S(1)}, u32[]{:S(2)}, u32[]{:S(2)}) %collective-permute-start.1) | collective-permute-done | bytes 639008 | tf_op jit(solution)/shard_map/ppermute | solution.py:17
  134.2 29.9 %collective-permute-done.2 = f32[8,39936]{1,0:T(8,128)S(1)} collective-permute-done((f32[8,39936]{1,0:T(8,128)S(1)}, f32[8,39936]{1,0:T(8,128)S(1)}, u32[]{:S(2)}, u32[]{:S(2)}) %collective-permute-start.2) | collective-permute-done | bytes 1277984 | tf_op jit(solution)/shard_map/ppermute | solution.py:17
  166.0 56.0 %collective-permute-done.3 = f32[16,39936]{1,0:T(8,128)} collective-permute-done((f32[16,39936]{1,0:T(8,128)S(1)}, f32[16,39936]{1,0:T(8,128)}, u32[]{:S(2)}, u32[]{:S(2)}) %collective-permute-start.3) | collective-permute-done | bytes 2555936 | tf_op jit(solution)/shard_map/ppermute | solution.py:17
  221.9 13.5 %concatenate.22 = f32[32,39936]{1,0:T(8,128)} concatenate(f32[2,39936]{1,0:T(2,128)S(1)} %reshape.30, f32[2,39936]{1,0:T(2,128)S(1)} %collective-permute-done, f32[4,39936]{1,0:T(4,128)S(1)} %collective-permute-done.1, f32[8,39936]{1,0:T(8,128)S(1)} %collective-permute-done.2, f32[16,39936]{1,0:T(8,128)} %collective-permute-done.3), dimensions={0} | concatenate | bytes 10223616 | tf_op jit(solution)/shard_map/concatenate | solution.py:66
  236.7 110.8 %collective-permute-done.4 = f32[32,39936]{1,0:T(8,128)} collective-permute-done((f32[32,39936]{1,0:T(8,128)}, f32[32,39936]{1,0:T(8,128)}, u32[]{:S(2)}, u32[]{:S(2)}) %collective-permute-start.4) | collective-permute-done | bytes 5111840 | tf_op jit(solution)/shard_map/ppermute | solution.py:17
  347.5 4.5 add.110
  358.4 13.3 %psum.91 = f32[32,32]{0,1:T(8,128)S(1)} all-reduce(f32[32,32]{0,1:T(8,128)S(1)} %fusion.194), channel_id=1, replica_groups=mesh['tm'=32,'slab'=4] {'slab'}, use_global_device_ids=true, to_apply=%region_2.3 | all-reduce | flops 1024 | bytes 8192 | tf_op jit(solution)/shard_map/psum | solution.py:43
  378.5 7.7 fusion.90
  386.2 26.0 %concatenate.23 = f32[64,39936]{1,0:T(8,128)} concatenate(f32[2,39936]{1,0:T(2,128)S(1)} %reshape.30, f32[2,39936]{1,0:T(2,128)S(1)} %collective-permute-done, f32[4,39936]{1,0:T(4,128)S(1)} %collective-permute-done.1, f32[8,39936]{1,0:T(8,128)S(1)} %collective-permute-done.2, f32[16,39936]{1,0:T(8,128)} %collective-permute-done.3, f32[32,39936]{1,0:T(8,128)} %collective-permute-done.4), dimensions={0} | concatenate | bytes 20447232 | tf_op jit(solution)/shard_map/concatenate | solution.py:53
  412.2 11.5 %fusion.195 = f32[32,64]{1,0:T(8,128)S(1)} fusion(f32[32,39936]{1,0:T(8,128)} %fusion.90, f32[64,39936]{1,0:T(8,128)} %concatenate.23), kind=kOutput, calls=%fused_computation.235 | convolution fusion | flops 981467136 | bytes 15343616 | tf_op jit(solution)/shard_map/dot_general | solution.py:39
  423.7 13.3 %psum.92 = f32[32,64]{1,0:T(8,128)S(1)} all-reduce(f32[32,64]{1,0:T(8,128)S(1)} %fusion.195), channel_id=1, replica_groups=mesh['tm'=32,'slab'=4] {'slab'}, use_global_device_ids=true, to_apply=%region_5.8 | all-reduce | flops 2048 | bytes 16384 | tf_op jit(solution)/shard_map/psum | solution.py:49
  437.0 7.9 fusion.196
  451.3 13.4 %psum.93 = f32[32,32]{0,1:T(8,128)S(1)} all-reduce(f32[32,32]{0,1:T(8,128)S(1)} %fusion.197), channel_id=1, replica_groups=mesh['tm'=32,'slab'=4] {'slab'}, use_global_device_ids=true, to_apply=%region_6.9 | all-reduce | flops 1024 | bytes 8192 | tf_op jit(solution)/shard_map/psum | solution.py:43
  471.5 6.4 fusion.87
  477.9 10.7 fusion.198
  488.6 13.6 %psum.94 = f32[32,64]{1,0:T(8,128)S(1)} all-reduce(f32[32,64]{1,0:T(8,128)S(1)} %fusion.198), channel_id=1, replica_groups=mesh['tm'=32,'slab'=4] {'slab'}, use_global_device_ids=true, to_apply=%region_7.10 | all-reduce | flops 2048 | bytes 16384 | tf_op jit(solution)/shard_map/psum | solution.py:49
  502.2 7.9 fusion.199
  516.6 13.3 %psum.95 = f32[32,32]{0,1:T(8,128)S(1)} all-reduce(f32[32,32]{0,1:T(8,128)S(1)} %fusion.200), channel_id=1, replica_groups=mesh['tm'=32,'slab'=4] {'slab'}, use_global_device_ids=true, to_apply=%region_8.11 | all-reduce | flops 1024 | bytes 8192 | tf_op jit(solution)/shard_map/psum | solution.py:43
  536.6 6.4 fusion.84
  543.0 10.7 fusion.201
  553.8 13.3 %psum.96 = f32[32,64]{1,0:T(8,128)S(1)} all-reduce(f32[32,64]{1,0:T(8,128)S(1)} %fusion.201), channel_id=1, replica_groups=mesh['tm'=32,'slab'=4] {'slab'}, use_global_device_ids=true, to_apply=%region_9.12 | all-reduce | flops 2048 | bytes 16384 | tf_op jit(solution)/shard_map/psum | solution.py:49
  567.1 7.9 fusion.202
  581.4 13.4 %psum.97 = f32[32,32]{0,1:T(8,128)S(1)} all-reduce(f32[32,32]{0,1:T(8,128)S(1)} %fusion.203), channel_id=1, replica_groups=mesh['tm'=32,'slab'=4] {'slab'}, use_global_device_ids=true, to_apply=%region_10.13 | all-reduce | flops 1024 | bytes 8192 | tf_op jit(solution)/shard_map/psum | solution.py:43
  601.6 6.4 fusion.81
  608.0 10.7 fusion.204
  618.7 13.6 %psum.98 = f32[32,64]{1,0:T(8,128)S(1)} all-reduce(f32[32,64]{1,0:T(8,128)S(1)} %fusion.204), channel_id=1, replica_groups=mesh['tm'=32,'slab'=4] {'slab'}, use_global_device_ids=true, to_apply=%region_11.14 | all-reduce | flops 2048 | bytes 16384 | tf_op jit(solution)/shard_map/psum | solution.py:49
  632.3 7.9 fusion.205
  646.7 13.3 %psum.99 = f32[32,32]{0,1:T(8,128)S(1)} all-reduce(f32[32,32]{0,1:T(8,128)S(1)} %fusion.206), channel_id=1, replica_groups=mesh['tm'=32,'slab'=4] {'slab'}, use_global_device_ids=true, to_apply=%region_12.15 | all-reduce | flops 1024 | bytes 8192 | tf_op jit(solution)/shard_map/psum | solution.py:43
  666.7 6.4 fusion.78
  675.5 10.7 fusion.207
  686.2 13.1 %psum.100 = f32[32,64]{1,0:T(8,128)S(1)} all-reduce(f32[32,64]{1,0:T(8,128)S(1)} %fusion.207), channel_id=1, replica_groups=mesh['tm'=32,'slab'=4] {'slab'}, use_global_device_ids=true, to_apply=%region_13.16 | all-reduce | flops 2048 | bytes 16384 | tf_op jit(solution)/shard_map/psum | solution.py:49
  703.2 8.4 convolution_select_fusion
  711.6 347.0 %all-reduce.2.cloned.1.call-done = f32[32,39936]{1,0:T(8,128)} async-done(((f32[32,39936]{1,0:T(8,128)}), f32[32,39936]{1,0:T(8,128)}) %all-reduce.2.cloned.1.call-update) | async-done | bytes 5111824 | tf_op jit(solution)/shard_map/psum | solution.py:22
  1058.6 7.1 fusion.209
  1065.7 13.3 %psum.102 = f32[32,32]{0,1:T(8,128)S(1)} all-reduce(f32[32,32]{0,1:T(8,128)S(1)} %fusion.209), channel_id=1, replica_groups=mesh['tm'=32,'slab'=4] {'slab'}, use_global_device_ids=true, to_apply=%region_15.18 | all-reduce | flops 1024 | bytes 8192 | tf_op jit(solution)/shard_map/psum | solution.py:43
  1085.8 6.4 fusion.74
  1098.5 7.1 psum.103
  1105.7 4.9 fusion.211
  (113 shorter events, 125.3 us)
Async XLA Ops:
  39.6 4.3 copy-start.7
  43.8 5.1 slice-start
  45.9 3.1 slice-start.1
  65.9 16.1 %all-to-all-start = ((bf16[4,2,39936]{2,1,0:T(2,128)(2,1)}), bf16[4,2,39936]{2,1,0:T(2,128)(2,1)}, u32[]{:S(2)}, u32[]{:S(2)}) async-start(bf16[4,2,39936]{2,1,0:T(2,128)(2,1)} %reshape.60), calls=%async_computation | async-start | bytes 1277952 | tf_op jit(solution)/shard_map/all_to_all | solution.py:91
  70.3 988.3 %all-reduce.2.cloned.1.call-start = ((), (), s32[]{:S(2)}) async-start(), calls=%async_computation.1 | async-start | bytes 10223616 | tf_op jit(solution)/shard_map/psum | solution.py:22
  95.0 6.6 copy-start.8
  95.0 6.6 copy-start.9
  104.3 11.0 collective-permute-start
  115.5 16.9 %collective-permute-start.1 = (f32[4,39936]{1,0:T(4,128)S(1)}, f32[4,39936]{1,0:T(4,128)S(1)}, u32[]{:S(2)}, u32[]{:S(2)}) collective-permute-start(f32[4,39936]{1,0:T(4,128)S(1)} %pad_maximum_fusion.3), channel_id=1, source_target_pairs={{8,0},{12,4},{16,8},{20,12},{24,16},{28,20},{32,24},{36,28},{40,32... | collective-permute-start | bytes 1916936 | tf_op jit(solution)/shard_map/ppermute | solution.py:17
  132.9 31.2 %collective-permute-start.2 = (f32[8,39936]{1,0:T(8,128)S(1)}, f32[8,39936]{1,0:T(8,128)S(1)}, u32[]{:S(2)}, u32[]{:S(2)}) collective-permute-start(f32[8,39936]{1,0:T(8,128)S(1)} %pad_maximum_fusion.1), channel_id=1, source_target_pairs={{16,0},{20,4},{24,8},{28,12},{32,16},{36,20},{40,24},{44,28},{48,3... | collective-permute-start | bytes 3833864 | tf_op jit(solution)/shard_map/ppermute | solution.py:17
  164.7 57.3 %collective-permute-start.3 = (f32[16,39936]{1,0:T(8,128)S(1)}, f32[16,39936]{1,0:T(8,128)}, u32[]{:S(2)}, u32[]{:S(2)}) collective-permute-start(f32[16,39936]{1,0:T(8,128)S(1)} %pad_maximum_fusion), channel_id=1, source_target_pairs={{32,0},{36,4},{40,8},{44,12},{48,16},{52,20},{56,24},{60,28},{64,3... | collective-permute-start | bytes 7667720 | tf_op jit(solution)/shard_map/ppermute | solution.py:17
  235.5 112.1 %collective-permute-start.4 = (f32[32,39936]{1,0:T(8,128)}, f32[32,39936]{1,0:T(8,128)}, u32[]{:S(2)}, u32[]{:S(2)}) collective-permute-start(f32[32,39936]{1,0:T(8,128)} %concatenate.22), channel_id=1, source_target_pairs={{64,0},{68,4},{72,8},{76,12},{80,16},{84,20},{88,24},{92,28},{96,3... | collective-permute-start | bytes 15335432 | tf_op jit(solution)/shard_map/ppermute | solution.py:17
  352.0 2.3 copy-start.4
  444.9 2.3 copy-start
  510.1 2.3 copy-start.1
  575.0 2.3 copy-start.2
  640.2 2.3 copy-start.3
  673.2 2.3 copy-start.5
  1092.2 2.3 copy-start.6
Sparse Core Ops, SparseCore 0:
  711.7 346.8 all-reduce.1
where the time goes:
time: 1120 us
  waiting for transfers between devices  577 us (52%)
  matrix products  193 us (17%)
  blocking collectives  154 us (14%)
  local copies, waits for them, and re-layouts  119 us (11%)
  other arithmetic  50.7 us (5%)
  between operations  14.2 us (1%)
    psum x1, waiting for transfers between devices, broadcast(): return lax.psum(kept, axis)  347 us
    ppermute x5, waiting for transfers between devices, shifted(): return lax.ppermute(shard, axis, pairs)  222 us
    dot_general x19, matrix products, matmul(): return jnp.dot(left, right, precision=lax.Precision.HIGHEST)  131 us
    psum x6, blocking collectives, orthonormal(): gram = lax.psum(matmul(rows, rows.T), 'slab')  80 us
    psum x5, blocking collectives, project_onto(): return lax.psum(matmul(qrows, stacked.T), 'slab')  67 us
    another operation x6, matrix products, orthonormal(): return lax.linalg.triangular_solve(factor, rows, left_side=True, lower=True)  39.7 us
    unnamed x26, local copies, waits for them, and re-layouts  27 us
    concatenate x1, local copies, waits for them, and re-layouts, truncate(): stacked = jnp.concatenate([lower_rows, upper_rows], axis=0)  26 us
  transfers between devices with their start and end apart: 7, of which 7 were waited for; matrix products, arithmetic and copies ran while one was open for 0% of the time, Pallas kernels for 0%

commit v1 on v0

--- a/solution.py
+++ b/solution.py
@@ -9,17 +9,6 @@
 RANK = 32
 ITERS = 4
 XW = 8
-
-
-def shifted(shard, axis, by):
-    size = lax.axis_size(axis)
-    pairs = [(i, i + by) for i in range(size) if 0 <= i + by < size]
-    return lax.ppermute(shard, axis, pairs)
-
-
-def broadcast(value, axis, source):
-    kept = jnp.where(lax.axis_index(axis) == source, value, 0).astype(value.dtype)
-    return lax.psum(kept, axis)
 
 
 def inverse_table(length, count, offset):
@@ -39,32 +28,9 @@
     return jnp.dot(left, right, precision=lax.Precision.HIGHEST)
 
 
-def orthonormal(rows):
-    gram = lax.psum(matmul(rows, rows.T), "slab")
-    factor = jnp.linalg.cholesky(gram)
+def orthonormal(rows, gram):
+    factor = jnp.linalg.cholesky(matmul(matmul(rows, gram), rows.T))
     return lax.linalg.triangular_solve(factor, rows, left_side=True, lower=True)
-
-
-def project_onto(qrows, stacked):
-    return lax.psum(matmul(qrows, stacked.T), "slab")
-
-
-def truncate(lower_rows, upper_rows):
-    stacked = jnp.concatenate([lower_rows, upper_rows], axis=0)
-    current = lower_rows + upper_rows
-    for sweep_index in range(ITERS):
-        qrows = orthonormal(current)
-        current = matmul(project_onto(qrows, stacked), stacked)
-    qrows = orthonormal(current)
-    correlation = project_onto(qrows, stacked)
-    coupling = jnp.linalg.cholesky(matmul(correlation, correlation.T))
-    return matmul(coupling.T, qrows)
-
-
-def merge_pair(lower_rows, upper_rows):
-    if 2 * lower_rows.shape[0] <= RANK:
-        return jnp.concatenate([lower_rows, upper_rows], axis=0)
-    return truncate(lower_rows, upper_rows)
 
 
 def local(kspace, sens):
@@ -102,16 +68,16 @@
     combined_real = jnp.sum(sens_real * depth_real + sens_other * depth_other, axis=1)
     combined_other = jnp.sum(sens_real * depth_other - sens_other * depth_real, axis=1)
     matrix = jnp.stack([combined_real, combined_other], axis=1).reshape(frames_dev, -1)
-    group_count = lax.axis_size("tm")
-    levels = group_count.bit_length() - 1
-    node_basis = matrix
-    for tier_index in range(levels):
-        partner = shifted(node_basis, "tm", -(2**tier_index))
-        node_basis = merge_pair(node_basis, partner)
-    node_basis = broadcast(node_basis, "tm", 0)
-    root_rows = orthonormal(node_basis)
-    loadings = lax.psum(matmul(root_rows, matrix.T), "slab")
-    projected = matmul(loadings.T, root_rows)
+    rows = lax.all_to_all(matrix, "tm", split_axis=1, concat_axis=0, tiled=True)
+    gram = lax.psum(matmul(rows, rows.T), ("tm", "slab"))
+    eye = jnp.eye(RANK, dtype=jnp.float32)
+    current = jnp.concatenate([eye, eye], axis=1)
+    for sweep_index in range(ITERS):
+        current = matmul(orthonormal(current, gram), gram)
+    coeff = orthonormal(current, gram)
+    mixing = matmul(matmul(coeff, gram).T, coeff)
+    projected = matmul(mixing, rows)
+    projected = lax.all_to_all(projected, "tm", split_axis=0, concat_axis=1, tiled=True)
     return projected.reshape(frames_dev, 2, XW, -1, NZ)
 
 

time: 1120 us -> 235 us (0.21)
  waiting for transfers between devices: 577 us -> 18.3 us
  matrix products: 193 us -> 26.8 us
  blocking collectives: 154 us -> 76.4 us
  local copies, waits for them, and re-layouts: 119 us -> 64.1 us
  other arithmetic: 50.7 us -> 34.6 us
  between operations: 14.2 us -> 0.48 us
    psum x1 -> x0, waiting for transfers between devices: 347 us -> none  [broadcast(): return lax.psum(kept, axis)]
    ppermute x5 -> x0, waiting for transfers between devices: 222 us -> none  [shifted(): return lax.ppermute(shard, axis, pairs)]
    dot_general x19 -> x18, matrix products: 131 us -> 3.36 us  [matmul(): return jnp.dot(left, right, precision=lax.Precision.HIGHEST)]
    psum x12 -> x1, blocking collectives: 154 us -> 62.4 us  [local(): gram = lax.psum(matmul(rows, rows.T), ('tm', 'slab'))]
    concatenate x2 -> x0, local copies, waits for them, and re-layouts: 39.5 us -> none  [the longest x1 26 us: truncate(): stacked = jnp.concatenate([lower_rows, upper_rows], axis=0)]
    another operation x6 -> x5, matrix products: 39.7 us -> 1.2 us  [orthonormal(): return lax.linalg.triangular_solve(factor, rows, left_side=True, lower=True)]
    unnamed x26 -> x12, local copies, waits for them, and re-layouts: 27 us -> 10.6 us
    all_to_all x0 -> x1, blocking collectives: none -> 14 us  [local(): lax.all_to_all(projected, 'tm', split_axis=0, concat_axis=1, tiled=True)]
  transfers between devices with their start and end apart: 7 -> 2, of which waited for: 7 -> 2; matrix products, arithmetic and copies ran while one was open for 0% -> 1% of each run, Pallas kernels for 0% -> 0%
where the time goes in v1:
time: 235 us; the launch traced here: 234 us
  blocking collectives  76.4 us (33%)
  local copies, waits for them, and re-layouts  64.1 us (27%)
  other arithmetic  34.6 us (15%)
  matrix products  26.8 us (11%)
  waiting for transfers between devices  18.3 us (8%)
  starting transfers between devices  13.7 us (6%)
    psum x1, blocking collectives, local(): gram = lax.psum(matmul(rows, rows.T), ('tm', 'slab'))  62.4 us
    dot_general x12, matrix products, contract(): jnp.einsum(pattern, matrix_table, operand, precision=lax.Precision.HIGHEST)  22.3 us
    another operation x16, other arithmetic, orthonormal(): factor = jnp.linalg.cholesky(matmul(matmul(rows, gram), rows.T))  18 us
    another operation x10, other arithmetic, orthonormal(): return lax.linalg.triangular_solve(factor, rows, left_side=True, lower=True)  15.4 us
    all_to_all x1, blocking collectives, local(): lax.all_to_all(projected, 'tm', split_axis=0, concat_axis=1, tiled=True)  14 us
    squeeze x1, local copies, waits for them, and re-layouts, local(): spectrum[1]  13.8 us
    squeeze x1, local copies, waits for them, and re-layouts, local(): spectrum[0]  13.7 us
    unnamed x12, local copies, waits for them, and re-layouts  10.6 us
  transfers between devices with their start and end apart: 2, of which 2 were waited for; matrix products, arithmetic and copies ran while one was open for 1% of the time, Pallas kernels for 0%

profile of v1, /device:TPU:0, one launch (start us, length us, event | category | flops | bytes accessed | tf_op | source)
XLA Modules:
  0.0 234.5 jit_solution(5598859404871233806)
XLA Ops:
  0.0 5.4 %fusion.180 = (bf16[1,2,4,24,9984]{4,3,2,1,0:T(8,128)(2,1)}, bf16[1,2,4,24,9984]{4,3,2,1,0:T(8,128)(2,1)}) fusion(bf16[2,2,4,24,9984]{4,3,2,1,0:T(8,128)(2,1)} %param.5), kind=kLoop, calls=%fused_computation.213 | loop fusion | bytes 15335424 | tf_op jit(solution)/shard_map/slice | solution.py:44
  5.4 13.7 %squeeze.16 = bf16[2,4,24,96,104]{4,3,2,1,0:T(8,128)(2,1)} reshape(bf16[1,2,4,24,9984]{4,3,2,1,0:T(8,128)(2,1)} %get-tuple-element.9) | data formatting | bytes 7667712 | tf_op jit(solution)/shard_map/squeeze | solution.py:44
  19.2 13.8 %squeeze.17 = bf16[2,4,24,96,104]{4,3,2,1,0:T(8,128)(2,1)} reshape(bf16[1,2,4,24,9984]{4,3,2,1,0:T(8,128)(2,1)} %get-tuple-element.10) | data formatting | bytes 7667712 | tf_op jit(solution)/shard_map/squeeze | solution.py:45
  33.0 4.3 %fusion.105 = f32[8,2,4,24,104]{4,0,3,2,1:T(8,128)S(1)} fusion(bf16[2,4,24,96,104]{4,3,2,1,0:T(8,128)(2,1)} %squeeze.16, s32[8]{0:T(128)S(1)} %iota_add_fusion), kind=kOutput, calls=%fused_computation.133 | convolution fusion | flops 184032768 | bytes 4472864 | tf_op jit(solution)/shard_map/jx,fczxy->fczjy/dot_general | solution.py:24
  37.3 2.1 fusion.103
  39.4 2.1 fusion.1
  41.4 1.0 fusion.10
  42.5 2.1 fusion
  44.5 1.0 fusion.6
  45.5 1.0 fusion.5
  46.5 1.0 fusion.4
  47.5 1.1 pad_maximum_fusion
  48.6 5.8 %copy.42 = bf16[2,2,4,24,8,104]{3,4,2,1,0,5:T(8,128)(2,1)S(1)} copy(bf16[2,2,4,24,8,104]{5,3,4,2,1,0:T(8,128)(2,1)} %pad_maximum_fusion) | data formatting | bytes 1277952 | tf_op jit(solution)/shard_map/stack | solution.py:56
  54.4 5.0 %reshape.64 = bf16[4,2,39936]{2,1,0:T(2,128)(2,1)} reshape(bf16[104,2,2,4,8,24]{5,4,3,2,1,0:T(8,128)(2,1)S(1)} %bitcast.164) | data formatting | bytes 1277952
  59.4 4.4 %all-to-all-start = ((bf16[4,2,39936]{2,1,0:T(2,128)(2,1)}), bf16[4,2,39936]{2,1,0:T(2,128)(2,1)}, u32[]{:S(2)}, u32[]{:S(2)}) async-start(bf16[4,2,39936]{2,1,0:T(2,128)(2,1)} %reshape.64), calls=%async_computation | async-start | bytes 1277952 | tf_op jit(solution)/shard_map/all_to_all | solution.py:57
  63.8 1.2 slice_bitcast_fusion.1
  65.0 0.9 copy.37
  65.9 0.9 copy.46
  66.8 8.7 %all-to-all-done = bf16[4,2,39936]{2,1,0:T(2,128)(2,1)} async-done(((bf16[4,2,39936]{2,1,0:T(2,128)(2,1)}), bf16[4,2,39936]{2,1,0:T(2,128)(2,1)}, u32[]{:S(2)}, u32[]{:S(2)}) %all-to-all-start) | async-done | bytes 639008 | tf_op jit(solution)/shard_map/all_to_all | solution.py:57
  75.5 5.6 %reshape.65 = bf16[104,2,2,4,8,24]{5,4,3,2,1,0:T(8,128)(2,1)S(1)} reshape(bf16[4,2,39936]{2,1,0:T(2,128)(2,1)} %all-to-all-done) | data formatting | bytes 1277952
  81.1 4.4 %copy.86 = bf16[2,2,4,24,8,4,26]{3,5,4,6,2,1,0:T(4,128)(2,1)S(1)} copy(bf16[2,2,4,24,8,4,26]{3,4,2,1,0,6,5:T(8,128)(2,1)S(1)} %bitcast.165) | data formatting | bytes 1277952 | tf_op jit(solution)/shard_map/all_to_all | solution.py:57
  85.5 1.2 fusion.181
  86.7 1.6 squeeze.18
  88.3 2.9 %fusion.16 = f32[2,4,8,26,96]{4,3,2,1,0:T(8,128)} fusion(bf16[2,4,96,8,26]{2,3,4,1,0:T(8,128)(2,1)} %squeeze.18), kind=kOutput, calls=%fused_computation.27 | convolution fusion | flops 184117248 | bytes 958464 | tf_op jit(solution)/shard_map/wz,fczxy->fcxyw/dot_general | solution.py:24
  91.1 0.9 squeeze.19
  92.0 0.8 fusion.12
  92.8 2.0 convolution_subtract_fusion
  94.9 2.2 add_reduce_fusion
  97.3 1.0 copy.49
  98.3 9.4 %all-to-all-start.1 = ((f32[2,32,1248]{2,0,1:T(2,128)}), f32[2,32,1248]{2,0,1:T(2,128)S(1)}, u32[]{:S(2)}, u32[]{:S(2)}) async-start(f32[2,32,1248]{2,0,1:T(2,128)} %copy.49), calls=%async_computation.1 | async-start | bytes 655360 | tf_op jit(solution)/shard_map/all_to_all | solution.py:71
  107.7 9.6 %all-to-all-done.1 = f32[2,32,1248]{2,0,1:T(2,128)S(1)} async-done(((f32[2,32,1248]{2,0,1:T(2,128)}), f32[2,32,1248]{2,0,1:T(2,128)S(1)}, u32[]{:S(2)}, u32[]{:S(2)}) %all-to-all-start.1) | async-done | bytes 319520 | tf_op jit(solution)/shard_map/all_to_all | solution.py:71
  118.2 62.4 %psum.7 = f32[64,64]{1,0:T(8,128)S(1)} all-reduce(f32[64,64]{1,0:T(8,128)S(1)} %fusion.182), channel_id=1, replica_groups=mesh['tm'=32,'slab'=4] {'tm','slab'}, use_global_device_ids=true, to_apply=%region_2.3 | all-reduce | flops 4096 | bytes 32768 | tf_op jit(solution)/shard_map/psum | solution.py:72
  181.1 2.9 %cholesky.89 = f32[32,32]{1,0:T(8,128)S(1)} custom-call(f32[32,32]{1,0:T(8,128)S(1)} %fusion.89), custom_call_target="Cholesky" | custom-call | tf_op jit(solution)/shard_map/jit(cholesky)/cholesky | solution.py:32
  184.7 0.7 fusion.70
  185.4 2.4 %custom-call.9 = f32[1,32,32]{1,2,0:T(8,128)S(1)} custom-call(f32[1,32,32]{2,1,0:T(8,128)S(1)} %fusion.70), custom_call_target="InvertDiagBlocksLowerTriangular" | custom-call | tf_op jit(solution)/shard_map/triangular_solve/custom-call.0 | solution.py:33
  188.6 2.9 %cholesky.100 = f32[32,32]{1,0:T(8,128)S(1)} custom-call(f32[32,32]{1,0:T(8,128)S(1)} %fusion.86), custom_call_target="Cholesky" | custom-call | tf_op jit(solution)/shard_map/jit(cholesky)/cholesky | solution.py:32
  192.2 0.7 fusion.71
  192.9 2.4 %custom-call.10 = f32[1,32,32]{1,2,0:T(8,128)S(1)} custom-call(f32[1,32,32]{2,1,0:T(8,128)S(1)} %fusion.71), custom_call_target="InvertDiagBlocksLowerTriangular" | custom-call | tf_op jit(solution)/shard_map/triangular_solve/custom-call.0 | solution.py:33
  196.1 2.9 %cholesky.111 = f32[32,32]{1,0:T(8,128)S(1)} custom-call(f32[32,32]{1,0:T(8,128)S(1)} %fusion.83), custom_call_target="Cholesky" | custom-call | tf_op jit(solution)/shard_map/jit(cholesky)/cholesky | solution.py:32
  199.7 0.7 fusion.72
  200.4 2.4 %custom-call.11 = f32[1,32,32]{1,2,0:T(8,128)S(1)} custom-call(f32[1,32,32]{2,1,0:T(8,128)S(1)} %fusion.72), custom_call_target="InvertDiagBlocksLowerTriangular" | custom-call | tf_op jit(solution)/shard_map/triangular_solve/custom-call.0 | solution.py:33
  203.6 2.9 %cholesky.122 = f32[32,32]{1,0:T(8,128)S(1)} custom-call(f32[32,32]{1,0:T(8,128)S(1)} %fusion.80), custom_call_target="Cholesky" | custom-call | tf_op jit(solution)/shard_map/jit(cholesky)/cholesky | solution.py:32
  207.2 0.7 fusion.73
  207.8 2.4 %custom-call.12 = f32[1,32,32]{1,2,0:T(8,128)S(1)} custom-call(f32[1,32,32]{2,1,0:T(8,128)S(1)} %fusion.73), custom_call_target="InvertDiagBlocksLowerTriangular" | custom-call | tf_op jit(solution)/shard_map/triangular_solve/custom-call.0 | solution.py:33
  211.1 2.9 %cholesky.133 = f32[32,32]{1,0:T(8,128)S(1)} custom-call(f32[32,32]{1,0:T(8,128)S(1)} %fusion.77), custom_call_target="Cholesky" | custom-call | tf_op jit(solution)/shard_map/jit(cholesky)/cholesky | solution.py:32
  215.3 2.4 %custom-call.13 = f32[1,32,32]{1,2,0:T(8,128)S(1)} custom-call(f32[1,32,32]{2,1,0:T(8,128)S(1)} %fusion.74), custom_call_target="InvertDiagBlocksLowerTriangular" | custom-call | tf_op jit(solution)/shard_map/triangular_solve/custom-call.0 | solution.py:33
  219.1 14.0 %all_to_all.47 = f32[32,2,1248]{2,1,0:T(2,128)S(1)} all-to-all(f32[32,2,1248]{2,1,0:T(2,128)S(1)} %copy.56), channel_id=1, replica_groups=mesh['tm'=32,'slab'=4] {'tm'}, dimensions={0} | all-to-all | bytes 638976 | tf_op jit(solution)/shard_map/all_to_all | solution.py:80
  233.4 1.0 copy.58
  (64 shorter events, 10.3 us)
Async XLA Ops:
  33.0 4.3 %copy-start = (bf16[2,4,24,96,104]{4,3,2,1,0:T(8,128)(2,1)S(1)}, bf16[2,4,24,96,104]{4,3,2,1,0:T(8,128)(2,1)}, u32[]{:S(2)}) copy-start(bf16[2,4,24,96,104]{4,3,2,1,0:T(8,128)(2,1)} %squeeze.17) | copy-start | bytes 11501572
  37.3 5.1 %slice-start = ((s8[4718592]{0:T(1024)(128)(4,1)}), s8[4194304]{0:T(1024)(128)(4,1)S(1)}, s32[]{:S(2)}) async-start(s8[4718592]{0:T(1024)(128)(4,1)} %bitcast.161), calls=%async_computation.3 | async-start | bytes 8388608
  39.4 3.1 %slice-start.1 = ((s8[4718592]{0:T(1024)(128)(4,1)}), s8[524288]{0:T(1024)(128)(4,1)S(1)}, s32[]{:S(2)}) async-start(s8[4718592]{0:T(1024)(128)(4,1)} %bitcast.161), calls=%async_computation.4 | async-start | bytes 1048576
  59.4 16.1 %all-to-all-start = ((bf16[4,2,39936]{2,1,0:T(2,128)(2,1)}), bf16[4,2,39936]{2,1,0:T(2,128)(2,1)}, u32[]{:S(2)}, u32[]{:S(2)}) async-start(bf16[4,2,39936]{2,1,0:T(2,128)(2,1)} %reshape.64), calls=%async_computation | async-start | bytes 1277952 | tf_op jit(solution)/shard_map/all_to_all | solution.py:57
  88.3 6.6 %copy-start.1 = (bf16[2,4,96,8,26]{2,3,4,1,0:T(8,128)(2,1)S(1)}, bf16[2,4,96,8,26]{2,3,4,1,0:T(8,128)(2,1)}, u32[]{:S(2)}) copy-start(bf16[2,4,96,8,26]{2,3,4,1,0:T(8,128)(2,1)} %squeeze.18) | copy-start | bytes 958468
  88.3 6.6 %copy-start.2 = (f32[4,8,26,96]{3,2,1,0:T(8,128)S(1)}, f32[4,8,26,96]{3,2,1,0:T(8,128)}, u32[]{:S(2)}) copy-start(f32[4,8,26,96]{3,2,1,0:T(8,128)} %copy.37) | copy-start | bytes 958468
  98.3 19.0 %all-to-all-start.1 = ((f32[2,32,1248]{2,0,1:T(2,128)}), f32[2,32,1248]{2,0,1:T(2,128)S(1)}, u32[]{:S(2)}, u32[]{:S(2)}) async-start(f32[2,32,1248]{2,0,1:T(2,128)} %copy.49), calls=%async_computation.1 | async-start | bytes 655360 | tf_op jit(solution)/shard_map/all_to_all | solution.py:71

commit v2 on v1

--- a/solution.py
+++ b/solution.py
@@ -1,6 +1,8 @@
 import jax
 import jax.numpy as jnp
 from jax import lax
+from jax.experimental import pallas as pl
+from jax.experimental.pallas import tpu as pltpu
 from jax.sharding import PartitionSpec as P
 
 NX = 96
@@ -9,6 +11,7 @@
 RANK = 32
 ITERS = 4
 XW = 8
+FRAMES = 64
 
 
 def inverse_table(length, count, offset):
@@ -28,9 +31,183 @@
     return jnp.dot(left, right, precision=lax.Precision.HIGHEST)
 
 
-def orthonormal(rows, gram):
-    factor = jnp.linalg.cholesky(matmul(matmul(rows, gram), rows.T))
-    return lax.linalg.triangular_solve(factor, rows, left_side=True, lower=True)
+def wait_bytes(ref, sem):
+    pltpu.make_async_copy(ref, ref, sem).wait()
+
+
+def eliminate(table, extra):
+    row = lax.broadcasted_iota(jnp.int32, (RANK, 1), 0)
+    for k in range(RANK):
+        pivot_row = table[k : k + 1, :]
+        factor = table[:, k : k + 1] * (1.0 / pivot_row[:, k : k + 1])
+        factor = jnp.where(row > k, factor, 0.0)
+        extra = extra - factor * extra[k : k + 1, :]
+        table = table - factor * pivot_row
+    lane = lax.broadcasted_iota(jnp.int32, (RANK, 128), 1)
+    rows = lax.broadcasted_iota(jnp.int32, (RANK, 128), 0)
+    diagonal = jnp.sum(jnp.where(lane == rows, table, 0.0), axis=1, keepdims=True)
+    scale = lax.rsqrt(diagonal)
+    return table * scale, extra * scale
+
+
+def dot_t(left, right):
+    return lax.dot_general(
+        left,
+        right,
+        (((1,), (1,)), ((), ())),
+        precision=lax.Precision.HIGHEST,
+        preferred_element_type=jnp.float32,
+    )
+
+
+def root_coefficients(gram):
+    def sweep(_, state):
+        weights, _ = state
+        image = matmul(weights, gram)
+        inner = dot_t(image, weights)
+        pad = jnp.zeros((RANK, 32), jnp.float32)
+        pad_wide = jnp.zeros((RANK, 64), jnp.float32)
+        table, extra = eliminate(
+            jnp.concatenate([inner, image, pad], axis=1),
+            jnp.concatenate([weights, pad_wide], axis=1),
+        )
+        return table[:, RANK : RANK + FRAMES], extra[:, :FRAMES]
+
+    lane = lax.broadcasted_iota(jnp.int32, (RANK, FRAMES), 1)
+    row = lax.broadcasted_iota(jnp.int32, (RANK, FRAMES), 0)
+    start = jnp.where(lane % RANK == row, 1.0, 0.0).astype(jnp.float32)
+    return lax.fori_loop(0, ITERS + 1, sweep, (start, start))
+
+
+def merge_kernel(flip, m_ref, out_ref, recv, whole, outf, outb, gx, gy, gz, sems):
+    me = lax.axis_index("tm")
+    slab = lax.axis_index("slab")
+    x_lo = me % 2
+    y_pos = (me // 2) % 4
+    z_pos = me // 8
+    owner = me + 1 - 2 * x_lo if flip else me
+    x_pos = slab * 2 + x_lo
+
+    def tm_peer(k):
+        return (lax.rem(me + k, 32), slab)
+
+    def x_peer(k):
+        other = lax.rem(x_pos + k, 8)
+        return (me - x_lo + other % 2, other // 2)
+
+    def y_peer(k):
+        return (z_pos * 8 + lax.rem(y_pos + k, 4) * 2 + x_lo, slab)
+
+    def z_peer(k):
+        return (lax.rem(z_pos + k, 4) * 8 + y_pos * 2 + x_lo, slab)
+
+    barrier = pltpu.get_barrier_semaphore()
+
+    def greet(peer):
+        pl.semaphore_signal(barrier, inc=1, device_id=peer, device_id_type=pl.DeviceIdType.MESH)
+
+    lax.fori_loop(1, 32, lambda k, c: (greet(tm_peer(k)), c)[1], 0)
+    lax.fori_loop(1, 8, lambda k, c: (greet(x_peer(k)), c)[1], 0)
+    pl.semaphore_wait(barrier, 38)
+
+    def send(src, dst, send_sem, recv_sem, peer):
+        pltpu.make_async_remote_copy(
+            src_ref=src,
+            dst_ref=dst,
+            send_sem=send_sem,
+            recv_sem=recv_sem,
+            device_id=peer,
+            device_id_type=pl.DeviceIdType.MESH,
+        ).start()
+
+    def scatter(k, c):
+        peer = tm_peer(k)
+        first = pl.multiple_of(peer[0] * 16, 16)
+        send(
+            m_ref.at[:, pl.ds(first, 16), :],
+            recv.at[pl.ds(2 * owner, 2)],
+            sems.at[0],
+            sems.at[1],
+            peer,
+        )
+        return c
+
+    lax.fori_loop(1, 32, scatter, 0)
+    mine = pl.multiple_of(me * 16, 16)
+    recv[pl.ds(2 * owner, 2)] = m_ref[:, pl.ds(mine, 16), :]
+    wait_bytes(m_ref.at[:, pl.ds(0, 31 * 16), :], sems.at[0])
+    wait_bytes(recv.at[pl.ds(0, 62)], sems.at[1])
+    flat = recv.reshape(FRAMES * 16, 128)
+    for i in range(16):
+        whole[:, i * 128 : (i + 1) * 128] = flat[pl.ds(i, FRAMES, stride=16), :]
+    gram = dot_t(whole[...], whole[...])
+    packed = jnp.concatenate([gram[:32], gram[32:]], axis=1)
+
+    def all_sum(value, buf, pos, count, peer_of, sem_at):
+        buf[pl.ds(pos, 1)] = value[None]
+        for k in range(1, count):
+            send(buf.at[pl.ds(pos, 1)], buf.at[pl.ds(pos, 1)], sems.at[sem_at], sems.at[sem_at + 1], peer_of(k))
+        wait_bytes(buf.at[pl.ds(0, count - 1)], sems.at[sem_at])
+        wait_bytes(buf.at[pl.ds(0, count - 1)], sems.at[sem_at + 1])
+        total = buf[0]
+        for k in range(1, count):
+            total = total + buf[k]
+        return total
+
+    packed = all_sum(packed, gx, x_pos, 8, x_peer, 2)
+    packed = all_sum(packed, gy, y_pos, 4, y_peer, 4)
+    packed = all_sum(packed, gz, z_pos, 4, z_peer, 6)
+    gram = jnp.concatenate([packed[:, :64], packed[:, 64:]], axis=0)
+    image, coeff = root_coefficients(gram)
+    mixing = lax.dot_general(
+        image,
+        coeff,
+        (((0,), (0,)), ((), ())),
+        precision=lax.Precision.HIGHEST,
+        preferred_element_type=jnp.float32,
+    )
+    for i in range(16):
+        outf[pl.ds(i, FRAMES, stride=16), :] = matmul(mixing, whole[:, i * 128 : (i + 1) * 128])
+    outb[...] = outf[...].reshape(FRAMES, 16, 128).astype(jnp.bfloat16)
+
+    def give(k, c):
+        peer = tm_peer(k)
+        send(
+            outb.at[pl.ds(2 * peer[0], 2)],
+            out_ref.at[:, pl.ds(mine, 16), :],
+            sems.at[8],
+            sems.at[9],
+            peer,
+        )
+        return c
+
+    lax.fori_loop(1, 32, give, 0)
+    out_ref[:, pl.ds(mine, 16), :] = outb[pl.ds(2 * me, 2)]
+    wait_bytes(outb.at[pl.ds(0, 62)], sems.at[8])
+    wait_bytes(out_ref.at[:, pl.ds(0, 31 * 16), :], sems.at[9])
+
+
+def merge(m, flip):
+    return pl.pallas_call(
+        lambda *refs: merge_kernel(flip, *refs),
+        out_shape=jax.ShapeDtypeStruct((2, 512, 128), jnp.bfloat16),
+        in_specs=[pl.BlockSpec(memory_space=pltpu.VMEM)],
+        out_specs=pl.BlockSpec(memory_space=pltpu.VMEM),
+        scratch_shapes=[
+            pltpu.VMEM((FRAMES, 16, 128), jnp.float32),
+            pltpu.VMEM((FRAMES, 2048), jnp.float32),
+            pltpu.VMEM((FRAMES * 16, 128), jnp.float32),
+            pltpu.VMEM((FRAMES, 16, 128), jnp.bfloat16),
+            pltpu.VMEM((8, 32, 128), jnp.float32),
+            pltpu.VMEM((4, 32, 128), jnp.float32),
+            pltpu.VMEM((4, 32, 128), jnp.float32),
+            pltpu.SemaphoreType.DMA((10,)),
+        ],
+        compiler_params=pltpu.CompilerParams(
+            collective_id=0, has_side_effects=True, vmem_limit_bytes=40 * 1024 * 1024
+        ),
+        name="merge",
+    )(m)
 
 
 def local(kspace, sens):
@@ -67,18 +244,11 @@
     sens_other = sens[1][None]
     combined_real = jnp.sum(sens_real * depth_real + sens_other * depth_other, axis=1)
     combined_other = jnp.sum(sens_real * depth_other - sens_other * depth_real, axis=1)
-    matrix = jnp.stack([combined_real, combined_other], axis=1).reshape(frames_dev, -1)
-    rows = lax.all_to_all(matrix, "tm", split_axis=1, concat_axis=0, tiled=True)
-    gram = lax.psum(matmul(rows, rows.T), ("tm", "slab"))
-    eye = jnp.eye(RANK, dtype=jnp.float32)
-    current = jnp.concatenate([eye, eye], axis=1)
-    for sweep_index in range(ITERS):
-        current = matmul(orthonormal(current, gram), gram)
-    coeff = orthonormal(current, gram)
-    mixing = matmul(matmul(coeff, gram).T, coeff)
-    projected = matmul(mixing, rows)
-    projected = lax.all_to_all(projected, "tm", split_axis=0, concat_axis=1, tiled=True)
-    return projected.reshape(frames_dev, 2, XW, -1, NZ)
+    matrix = jnp.stack([combined_real, combined_other], axis=1).transpose(0, 3, 1, 2, 4)
+    matrix = jnp.pad(matrix, ((0, 0), (0, 6), (0, 0), (0, 0), (0, 32))).reshape(2, 512, 128)
+    projected = merge(matrix, False).reshape(2, 32, 2, XW, 128)
+    projected = projected[:, :26, :, :, :NZ].astype(jnp.float32)
+    return projected.transpose(0, 2, 3, 1, 4)
 
 
 def solution(mesh):

time: 235 us -> 147 us (0.63)
  blocking collectives: 76.4 us -> 0 us
  Pallas kernels: 0 us -> 48.4 us
  other arithmetic: 34.6 us -> 1.89 us
  waiting for transfers between devices: 18.3 us -> 8.69 us
  starting transfers between devices: 13.7 us -> 4.38 us
  matrix products: 26.8 us -> 22.3 us
  local copies, waits for them, and re-layouts: 64.1 us -> 60.8 us
    psum x1 -> x0, blocking collectives: 62.4 us -> none  [local(): gram = lax.psum(matmul(rows, rows.T), ('tm', 'slab'))]
    pallas_call x0 -> x1, Pallas kernels: none -> 48.4 us  [merge(): pl.pallas_call(lambda *refs: merge_kernel(flip, *refs), out_shape=jax.Sha...]
    another operation x27 -> x0, other arithmetic: 33.5 us -> none  [the longest x16 18 us: orthonormal(): factor = jnp.linalg.cholesky(matmul(matmul(rows, gram), rows.T))]
    all_to_all x1 -> x0, blocking collectives: 14 us -> none  [local(): lax.all_to_all(projected, 'tm', split_axis=0, concat_axis=1, tiled=True)]
    all_to_all x1 -> x0, waiting for transfers between devices: 9.63 us -> none  [local(): rows = lax.all_to_all(matrix, 'tm', split_axis=1, concat_axis=0, tiled=True)]
    all_to_all x1 -> x0, starting transfers between devices: 9.35 us -> none  [local(): rows = lax.all_to_all(matrix, 'tm', split_axis=1, concat_axis=0, tiled=True)]
    dot_general x18 -> x0, matrix products: 3.36 us -> none  [matmul(): return jnp.dot(left, right, precision=lax.Precision.HIGHEST)]
    unnamed x12 -> x13, local copies, waits for them, and re-layouts: 10.6 us -> 10.9 us
  transfers between devices with their start and end apart: 2 -> 1, of which waited for: 2 -> 1; matrix products, arithmetic and copies ran while one was open for 1% -> 2% of each run, Pallas kernels for 0% -> 0%
where the time goes in v2:
time: 147 us
  local copies, waits for them, and re-layouts  60.8 us (41%)
  Pallas kernels  48.4 us (33%)
  matrix products  22.3 us (15%)
  waiting for transfers between devices  8.69 us (6%)
  starting transfers between devices  4.38 us (3%)
  other arithmetic  1.89 us (1%)
    pallas_call x1, Pallas kernels, merge(): pl.pallas_call(lambda *refs: merge_kernel(flip, *refs), out_shape=jax.Sha...  48.4 us
    dot_general x12, matrix products, contract(): jnp.einsum(pattern, matrix_table, operand, precision=lax.Precision.HIGHEST)  22.3 us
    squeeze x1, local copies, waits for them, and re-layouts, local(): spectrum[1]  13.8 us
    squeeze x1, local copies, waits for them, and re-layouts, local(): spectrum[0]  13.8 us
    unnamed x13, local copies, waits for them, and re-layouts  10.9 us
    all_to_all x1, waiting for transfers between devices, local(): lax.all_to_all(planes, 'slab', split_axis=5, concat_axis=3, tiled=True)  8.69 us
    another operation x1, local copies, waits for them, and re-layouts, local(): planes = jnp.stack([down_real, down_other]).astype(jnp.bfloat16)  5.79 us
    slice x1, local copies, waits for them, and re-layouts, local(): spectrum[0]  5.46 us
  transfers between devices with their start and end apart: 1, of which 1 were waited for; matrix products, arithmetic and copies ran while one was open for 2% of the time, Pallas kernels for 0%

profile of v2, /device:TPU:0, one launch (start us, length us, event | category | flops | bytes accessed | tf_op | source)
XLA Modules:
  0.0 146.6 jit_solution(5247865724918053423)
XLA Ops:
  0.0 5.5 %fusion.147 = (bf16[1,2,4,24,9984]{4,3,2,1,0:T(8,128)(2,1)}, bf16[1,2,4,24,9984]{4,3,2,1,0:T(8,128)(2,1)}) fusion(bf16[2,2,4,24,9984]{4,3,2,1,0:T(8,128)(2,1)} %param.2), kind=kLoop, calls=%fused_computation.162 | loop fusion | bytes 15335424 | tf_op jit(solution)/shard_map/slice | solution.py:221
  5.5 13.8 %squeeze.16 = bf16[2,4,24,96,104]{4,3,2,1,0:T(8,128)(2,1)} reshape(bf16[1,2,4,24,9984]{4,3,2,1,0:T(8,128)(2,1)} %get-tuple-element.7) | data formatting | bytes 7667712 | tf_op jit(solution)/shard_map/squeeze | solution.py:221
  19.2 13.8 %squeeze.17 = bf16[2,4,24,96,104]{4,3,2,1,0:T(8,128)(2,1)} reshape(bf16[1,2,4,24,9984]{4,3,2,1,0:T(8,128)(2,1)} %get-tuple-element.8) | data formatting | bytes 7667712 | tf_op jit(solution)/shard_map/squeeze | solution.py:222
  33.0 0.0 copy-start
  33.0 4.3 %fusion.74 = f32[8,2,4,24,104]{4,0,3,2,1:T(8,128)S(1)} fusion(bf16[2,4,24,96,104]{4,3,2,1,0:T(8,128)(2,1)} %squeeze.16, s32[8]{0:T(128)S(1)} %iota_add_fusion), kind=kOutput, calls=%fused_computation.89 | convolution fusion | flops 184032768 | bytes 4472864 | tf_op jit(solution)/shard_map/jx,fczxy->fczjy/dot_general | solution.py:27
  37.3 0.0 copy-done
  37.3 0.0 slice-start
  37.3 2.1 %fusion.72 = f32[8,2,4,24,104]{4,0,3,2,1:T(8,128)S(1)} fusion(bf16[2,4,24,96,104]{4,3,2,1,0:T(8,128)(2,1)S(1)} %copy-done, s32[8]{0:T(128)S(1)} %iota_add_fusion), kind=kOutput, calls=%fused_computation.87 | convolution fusion | flops 184032768 | bytes 4472864 | tf_op jit(solution)/shard_map/jx,fczxy->fczjy/dot_general | solution.py:27
  39.4 0.0 slice-start.1
  39.4 2.1 %fusion.1 = f32[2,4,24,8,104]{4,3,2,1,0:T(8,128)S(1)} fusion(f32[8,2,4,24,104]{4,0,3,2,1:T(8,128)S(1)} %fusion.74, bf16[2,4,24,96,104]{4,3,2,1,0:T(8,128)(2,1)S(1)} %copy-done, s32[8]{0:T(128)S(1)} %iota_add_fusion), kind=kOutput, calls=%fused_computation.8 | convolution fusion | flops 184192512 | bytes 5111840 | tf_op jit(solution)/shard_map/jx,fczxy->fczjy/dot_general | solution.py:27
  41.4 1.0 fusion.10
  42.4 0.0 slice-done
  42.4 0.0 slice-done.1
  42.5 2.1 %fusion = f32[2,4,24,8,104]{4,3,2,1,0:T(8,128)S(1)} fusion(f32[8,2,4,24,104]{4,0,3,2,1:T(8,128)S(1)} %fusion.72, bf16[2,4,24,96,104]{4,3,2,1,0:T(8,128)(2,1)S(1)} %bitcast.85, s32[8]{0:T(128)S(1)} %iota_add_fusion), kind=kOutput, calls=%fused_computation.6 | convolution fusion | flops 184192512 | bytes 5111840 | tf_op jit(solution)/shard_map/jx,fczxy->fczjy/dot_general | solution.py:27
  44.5 1.0 fusion.6
  45.5 1.0 fusion.5
  46.5 1.0 fusion.4
  47.5 1.1 pad_maximum_fusion
  48.6 5.8 %copy.29 = bf16[2,2,4,24,8,104]{3,4,2,1,0,5:T(8,128)(2,1)S(1)} copy(bf16[2,2,4,24,8,104]{5,3,4,2,1,0:T(8,128)(2,1)} %pad_maximum_fusion) | data formatting | bytes 1277952 | tf_op jit(solution)/shard_map/stack | solution.py:233
  54.4 5.0 %reshape.27 = bf16[4,2,39936]{2,1,0:T(2,128)(2,1)} reshape(bf16[104,2,2,4,8,24]{5,4,3,2,1,0:T(8,128)(2,1)S(1)} %bitcast.87) | data formatting | bytes 1277952
  59.4 4.4 %all-to-all-start = ((bf16[4,2,39936]{2,1,0:T(2,128)(2,1)}), bf16[4,2,39936]{2,1,0:T(2,128)(2,1)}, u32[]{:S(2)}, u32[]{:S(2)}) async-start(bf16[4,2,39936]{2,1,0:T(2,128)(2,1)} %reshape.27), calls=%async_computation | async-start | bytes 1277952 | tf_op jit(solution)/shard_map/all_to_all | solution.py:234
  63.8 1.2 slice_bitcast_fusion.1
  65.0 0.9 copy.24
  65.9 0.9 copy.33
  66.8 8.7 %all-to-all-done = bf16[4,2,39936]{2,1,0:T(2,128)(2,1)} async-done(((bf16[4,2,39936]{2,1,0:T(2,128)(2,1)}), bf16[4,2,39936]{2,1,0:T(2,128)(2,1)}, u32[]{:S(2)}, u32[]{:S(2)}) %all-to-all-start) | async-done | bytes 639008 | tf_op jit(solution)/shard_map/all_to_all | solution.py:234
  75.5 5.6 %reshape.28 = bf16[104,2,2,4,8,24]{5,4,3,2,1,0:T(8,128)(2,1)S(1)} reshape(bf16[4,2,39936]{2,1,0:T(2,128)(2,1)} %all-to-all-done) | data formatting | bytes 1277952
  81.1 4.4 %copy.66 = bf16[2,2,4,24,8,4,26]{3,5,4,6,2,1,0:T(4,128)(2,1)S(1)} copy(bf16[2,2,4,24,8,4,26]{3,4,2,1,0,6,5:T(8,128)(2,1)S(1)} %bitcast.88) | data formatting | bytes 1277952 | tf_op jit(solution)/shard_map/all_to_all | solution.py:234
  85.5 1.2 fusion.148
  86.7 1.6 %squeeze.18 = bf16[2,4,96,8,26]{2,3,4,1,0:T(8,128)(2,1)} reshape(bf16[1,2,4,4,24,8,26]{4,3,5,6,2,1,0:T(4,128)(2,1)S(1)} %get-tuple-element.9) | data formatting | bytes 638976 | tf_op jit(solution)/shard_map/squeeze | solution.py:237
  88.3 0.0 copy-start.1
  88.3 0.0 copy-start.2
  88.3 2.8 %fusion.16 = f32[2,4,8,26,96]{4,3,2,1,0:T(8,128)} fusion(bf16[2,4,96,8,26]{2,3,4,1,0:T(8,128)(2,1)} %squeeze.18), kind=kOutput, calls=%fused_computation.27 | convolution fusion | flops 184117248 | bytes 958464 | tf_op jit(solution)/shard_map/wz,fczxy->fcxyw/dot_general | solution.py:27
  91.1 0.9 squeeze.19
  92.0 0.8 fusion.12
  92.8 2.0 %convolution_subtract_fusion = f32[2,4,8,26,96]{4,3,2,1,0:T(8,128)S(1)} fusion(f32[2,4,8,26,96]{4,3,2,1,0:T(8,128)} %fusion.16, bf16[2,4,96,8,26]{2,3,4,1,0:T(8,128)(2,1)S(1)} %squeeze.19), kind=kOutput, calls=%fused_computation.2 | convolution fusion | flops 184276992 | bytes 1597440 | tf_op jit(solution)/shard_map/wz,fczxy->fcxyw/dot_general | solution.py:27
  94.8 0.0 copy-done.1
  94.8 0.0 copy-done.2
  94.8 2.2 %add_reduce_fusion = (f32[2,8,26,96]{3,2,1,0:T(8,128)S(1)}, f32[2,8,26,96]{3,2,1,0:T(8,128)S(1)}) fusion(f32[2,4,8,26,96]{4,3,2,1,0:T(8,128)S(1)} %convolution_subtract_fusion, f32[4,8,26,96]{3,2,1,0:T(8,128)} %copy.33, f32[4,8,26,96]{3,2,1,0:T(8,128)S(1)} %copy-done.2, f32[2,4,8,26,96]{4,3,2,1,0:T(8,128)S(1)} %fusion.12, ...), kind=kOutput, calls=%fused_computation.14 | convolution fusion | flops 185475072 | bytes 2555904 | tf_op jit(solution)/shard_map/wz,fczxy->fcxyw/dot_general | solution.py:27
  97.1 0.3 copy.45
  97.4 48.4 %merge.1 = bf16[2,512,128]{2,1,0:T(8,128)(2,1)S(1)} custom-call(f32[2,512,128]{2,1,0:T(8,128)S(1)} %bitcast.82), custom_call_target="tpu_custom_call" | custom-call | tf_op jit(solution)/shard_map/merge/pallas_call | solution.py:191
  145.8 0.8 convert_bitcast_fusion
  (4 shorter events, 0.1 us)
Async XLA Ops:
  33.0 4.3 %copy-start = (bf16[2,4,24,96,104]{4,3,2,1,0:T(8,128)(2,1)S(1)}, bf16[2,4,24,96,104]{4,3,2,1,0:T(8,128)(2,1)}, u32[]{:S(2)}) copy-start(bf16[2,4,24,96,104]{4,3,2,1,0:T(8,128)(2,1)} %squeeze.17) | copy-start | bytes 11501572
  37.3 5.1 %slice-start = ((s8[4718592]{0:T(1024)(128)(4,1)}), s8[4194304]{0:T(1024)(128)(4,1)S(1)}, s32[]{:S(2)}) async-start(s8[4718592]{0:T(1024)(128)(4,1)} %bitcast.84), calls=%async_computation.1 | async-start | bytes 8388608
  39.4 3.1 %slice-start.1 = ((s8[4718592]{0:T(1024)(128)(4,1)}), s8[524288]{0:T(1024)(128)(4,1)S(1)}, s32[]{:S(2)}) async-start(s8[4718592]{0:T(1024)(128)(4,1)} %bitcast.84), calls=%async_computation.2 | async-start | bytes 1048576
  59.4 16.1 %all-to-all-start = ((bf16[4,2,39936]{2,1,0:T(2,128)(2,1)}), bf16[4,2,39936]{2,1,0:T(2,128)(2,1)}, u32[]{:S(2)}, u32[]{:S(2)}) async-start(bf16[4,2,39936]{2,1,0:T(2,128)(2,1)} %reshape.27), calls=%async_computation | async-start | bytes 1277952 | tf_op jit(solution)/shard_map/all_to_all | solution.py:234
  88.3 6.5 %copy-start.1 = (bf16[2,4,96,8,26]{2,3,4,1,0:T(8,128)(2,1)S(1)}, bf16[2,4,96,8,26]{2,3,4,1,0:T(8,128)(2,1)}, u32[]{:S(2)}) copy-start(bf16[2,4,96,8,26]{2,3,4,1,0:T(8,128)(2,1)} %squeeze.18) | copy-start | bytes 958468
  88.3 6.6 %copy-start.2 = (f32[4,8,26,96]{3,2,1,0:T(8,128)S(1)}, f32[4,8,26,96]{3,2,1,0:T(8,128)}, u32[]{:S(2)}) copy-start(f32[4,8,26,96]{3,2,1,0:T(8,128)} %copy.24) | copy-start | bytes 958468

commit v3 on v2

--- a/solution.py
+++ b/solution.py
@@ -1,5 +1,7 @@
 import jax
 import jax.numpy as jnp
+import ml_dtypes
+import numpy as np
 from jax import lax
 from jax.experimental import pallas as pl
 from jax.experimental.pallas import tpu as pltpu
@@ -12,19 +14,6 @@
 ITERS = 4
 XW = 8
 FRAMES = 64
-
-
-def inverse_table(length, count, offset):
-    outputs = jnp.arange(count, dtype=jnp.int32) + offset
-    inputs = jnp.arange(length, dtype=jnp.int32)
-    phase = outputs[:, None] * inputs[None, :] % length
-    angle = phase.astype(jnp.float32) * (2.0 * jnp.pi / length)
-    norm_factor = 1.0 / jnp.sqrt(jnp.float32(length))
-    return (jnp.cos(angle) * norm_factor, jnp.sin(angle) * norm_factor)
-
-
-def contract(pattern, matrix_table, operand):
-    return jnp.einsum(pattern, matrix_table, operand, precision=lax.Precision.HIGHEST)
 
 
 def matmul(left, right):
@@ -210,43 +199,210 @@
     )(m)
 
 
+def split_bf16(table):
+    high = table.astype(ml_dtypes.bfloat16)
+    low = (table - high.astype(np.float64)).astype(ml_dtypes.bfloat16)
+    return high, low
+
+
+def across_table():
+    x = np.arange(XW) + (NX - XW) // 2
+    angle = 2.0 * np.pi * (x[:, None] * np.arange(NX)[None, :] % NX) / NX
+    cos, sin = np.cos(angle) / np.sqrt(NX), np.sin(angle) / np.sqrt(NX)
+    table = np.zeros((XW, 2, 8, NX, 2, 8))
+    for r in range(8):
+        table[:, 0, r, :, 0, r] = cos
+        table[:, 0, r, :, 1, r] = -sin
+        table[:, 1, r, :, 0, r] = sin
+        table[:, 1, r, :, 1, r] = cos
+    return np.concatenate(split_bf16(table.reshape(XW * 16, NX * 16)), axis=0)
+
+
+def down_table():
+    angle = 2.0 * np.pi * (np.arange(NY)[:, None] * np.arange(NY)[None, :] % NY) / NY
+    table = np.zeros((4, 32, 2, 128))
+    table[:, :26, 0, :NY] = np.cos(angle).reshape(4, 26, NY) / np.sqrt(NY)
+    table[:, :26, 1, :NY] = np.sin(angle).reshape(4, 26, NY) / np.sqrt(NY)
+    return np.concatenate(split_bf16(table.reshape(128, 256)), axis=0)
+
+
+def depth_table():
+    angle = 2.0 * np.pi * (np.arange(NZ)[:, None] * np.arange(NZ)[None, :] % NZ) / NZ
+    cos = (np.cos(angle) / np.sqrt(NZ)).reshape(4, 24, NZ)
+    sin = (np.sin(angle) / np.sqrt(NZ)).reshape(4, 24, NZ)
+    table = np.zeros((4, 2, 4, 24, 4, 2, 128))
+    for c in range(4):
+        table[:, 0, c, :, c, 0, :NZ] = cos
+        table[:, 1, c, :, c, 0, :NZ] = -sin
+        table[:, 0, c, :, c, 1, :NZ] = sin
+        table[:, 1, c, :, c, 1, :NZ] = cos
+    full = np.zeros((4, 320, 1024))
+    full[:, 64:256] = table.reshape(4, 192, 1024)
+    return np.stack(split_bf16(full))
+
+
+def front_kernel(
+    k_ref, sens_ref, across_ref, down_ref, depth_ref, m_ref,
+    data, spec_hi, spec_lo, sent, got, depth, acc, data_sems, depth_sem, sems,
+):
+    me = lax.axis_index("tm")
+    slab = lax.axis_index("slab")
+    mirror = me + 1 - 2 * (me % 2)
+
+    def fetch(g):
+        rows = pl.ds(pl.multiple_of(g * 16, 16), 16)
+        return pltpu.make_async_copy(k_ref.at[:, rows, :], data.at[:, rows, :], data_sems.at[g])
+
+    def begin(g, c):
+        fetch(g).start()
+        return c
+
+    lax.fori_loop(0, 12, begin, 0)
+    depth_copy = pltpu.make_async_copy(depth_ref, depth, depth_sem)
+    depth_copy.start()
+    barrier = pltpu.get_barrier_semaphore()
+    for s in range(4):
+        pl.semaphore_signal(
+            barrier, inc=1, device_id=(mirror, s), device_id_type=pl.DeviceIdType.MESH
+        )
+    m_ref[...] = jnp.zeros_like(m_ref)
+
+    def across(g, c):
+        fetch(g).wait()
+        rows = pl.ds(pl.multiple_of(g * 16, 16), 16)
+        place = pl.multiple_of(lax.rem(g, 6) * 16, 16)
+        total = jnp.zeros((256, 256), jnp.float32)
+        for t in range(6):
+            lo, hi = t * 1664, (t + 1) * 1664
+            real = data[0, rows, lo:hi].astype(jnp.float32)
+            other = data[1, rows, lo:hi].astype(jnp.float32)
+            parts = []
+            for h in range(2):
+                both = jnp.concatenate(
+                    [real[h * 8 : h * 8 + 8], other[h * 8 : h * 8 + 8]], axis=0
+                ).astype(jnp.bfloat16)
+                both = jnp.concatenate([both, jnp.zeros((16, 128), jnp.bfloat16)], axis=1)
+                parts.append(
+                    jnp.concatenate([both[:, a * 104 : a * 104 + 128] for a in range(16)], axis=0)
+                )
+            total = total + jnp.dot(
+                across_ref[:, t * 256 : (t + 1) * 256],
+                jnp.concatenate(parts, axis=1),
+                preferred_element_type=jnp.float32,
+            )
+        image = total[:128] + total[128:]
+        for j in range(XW):
+            real = jnp.concatenate([image[j * 16 : j * 16 + 8, h * 128 : h * 128 + 128] for h in range(2)], axis=0)
+            other = jnp.concatenate([image[j * 16 + 8 : j * 16 + 16, h * 128 : h * 128 + 128] for h in range(2)], axis=0)
+            for part, pair in ((0, (real, -other)), (1, (other, real))):
+                value = jnp.concatenate(pair, axis=1)
+                high = value.astype(jnp.bfloat16)
+                low = (value - high.astype(jnp.float32)).astype(jnp.bfloat16)
+                at = pl.ds(place + ((j % 2) * 192 + part * 96), 16)
+                spec_hi[j // 2, at, :] = high
+                spec_lo[j // 2, at, :] = low
+        return c
+
+    def down(f):
+        for jp in range(4):
+            dims = (((1,), (1,)), ((), ()))
+            first = lax.dot_general(down_ref[...], spec_hi[jp], dims, preferred_element_type=jnp.float32)
+            second = lax.dot_general(down_ref[:128, :], spec_lo[jp], dims, preferred_element_type=jnp.float32)
+            planes = (first[:128] + first[128:] + second).astype(jnp.bfloat16)
+            for s in range(4):
+                sent[f, s, jp * 32 : jp * 32 + 32, :] = planes[s * 32 : s * 32 + 32]
+
+    def copy(f, s):
+        return pltpu.make_async_remote_copy(
+            src_ref=sent.at[f, s],
+            dst_ref=got.at[f, slab],
+            send_sem=sems.at[f],
+            recv_sem=sems.at[2 + f],
+            device_id=(mirror, s),
+            device_id_type=pl.DeviceIdType.MESH,
+        )
+
+    for f in range(2):
+        lax.fori_loop(6 * f, 6 * f + 6, across, 0)
+        down(f)
+        if f == 0:
+            pl.semaphore_wait(barrier, 4)
+        for s in range(4):
+            copy(f, s).start()
+    depth_copy.wait()
+    for f in range(2):
+        wait_bytes(got.at[f], sems.at[2 + f])
+        for j2 in range(2):
+            total = None
+            for q in range(4):
+                window = got[f, q, :, j2 * 128 : j2 * 128 + 256]
+                for h in range(2):
+                    term = jnp.dot(
+                        window,
+                        depth[h, q, 64 - 64 * j2 : 320 - 64 * j2, :],
+                        preferred_element_type=jnp.float32,
+                    )
+                    total = term if total is None else total + term
+            acc[...] = total
+
+            def combine(jp, c, j2=j2, f=f):
+                j = jp * 2 + j2
+                real = other = None
+                for coil in range(4):
+                    rows = pl.ds(pl.multiple_of(jp * 32, 32), 32)
+                    wave_real = acc[rows, coil * 256 : coil * 256 + 96][:26]
+                    wave_other = acc[rows, coil * 256 + 128 : coil * 256 + 224][:26]
+                    sens_real = sens_ref[0, coil, pl.ds(j, 26, stride=8), :]
+                    sens_other = sens_ref[1, coil, pl.ds(j, 26, stride=8), :]
+                    term_real = sens_real * wave_real + sens_other * wave_other
+                    term_other = sens_real * wave_other - sens_other * wave_real
+                    real = term_real if real is None else real + term_real
+                    other = term_other if other is None else other + term_other
+                pad = ((0, 0), (0, 32))
+                m_ref[f, pl.ds(j, 26, stride=16), :] = jnp.pad(real, pad)
+                m_ref[f, pl.ds(j + 8, 26, stride=16), :] = jnp.pad(other, pad)
+                return c
+
+            lax.fori_loop(0, 4, combine, 0)
+    for f in range(2):
+        wait_bytes(sent.at[f], sems.at[f])
+
+
+def front(kspace, sens):
+    any_spec = pl.BlockSpec(memory_space=pl.ANY)
+    vmem_spec = pl.BlockSpec(memory_space=pltpu.VMEM)
+    return pl.pallas_call(
+        front_kernel,
+        out_shape=jax.ShapeDtypeStruct((2, 512, 128), jnp.float32),
+        in_specs=[any_spec, vmem_spec, vmem_spec, vmem_spec, any_spec],
+        out_specs=vmem_spec,
+        scratch_shapes=[
+            pltpu.VMEM((2, 192, 9984), jnp.bfloat16),
+            pltpu.VMEM((4, 384, 256), jnp.bfloat16),
+            pltpu.VMEM((4, 384, 256), jnp.bfloat16),
+            pltpu.VMEM((2, 4, 128, 384), jnp.bfloat16),
+            pltpu.VMEM((2, 4, 128, 384), jnp.bfloat16),
+            pltpu.VMEM((2, 4, 320, 1024), jnp.bfloat16),
+            pltpu.VMEM((128, 1024), jnp.float32),
+            pltpu.SemaphoreType.DMA((12,)),
+            pltpu.SemaphoreType.DMA,
+            pltpu.SemaphoreType.DMA((4,)),
+        ],
+        compiler_params=pltpu.CompilerParams(
+            collective_id=1, has_side_effects=True, vmem_limit_bytes=48 * 1024 * 1024
+        ),
+        name="front",
+    )(
+        kspace.reshape(2, 192, NX * NY),
+        sens.transpose(0, 1, 3, 2, 4).reshape(2, 4, 208, NZ),
+        across_table(),
+        down_table(),
+        depth_table(),
+    )
+
+
 def local(kspace, sens):
-    frames_dev = kspace.shape[1]
-    coil_count = kspace.shape[2]
-    depth_dev = kspace.shape[3]
-    spectrum = kspace.astype(jnp.float32).reshape(2, frames_dev, coil_count, depth_dev, NX, NY)
-    across_cos, across_sin = inverse_table(NX, XW, (NX - XW) // 2)
-    down_cos, down_sin = inverse_table(NY, NY, 0)
-    depth_cos, depth_sin = inverse_table(NZ, NZ, 0)
-    across_real = contract("jx,fczxy->fczjy", across_cos, spectrum[0]) - contract(
-        "jx,fczxy->fczjy", across_sin, spectrum[1]
-    )
-    across_other = contract("jx,fczxy->fczjy", across_cos, spectrum[1]) + contract(
-        "jx,fczxy->fczjy", across_sin, spectrum[0]
-    )
-    down_real = contract("my,fczjy->fczjm", down_cos, across_real) - contract(
-        "my,fczjy->fczjm", down_sin, across_other
-    )
-    down_other = contract("my,fczjy->fczjm", down_cos, across_other) + contract(
-        "my,fczjy->fczjm", down_sin, across_real
-    )
-    planes = jnp.stack([down_real, down_other]).astype(jnp.bfloat16)
-    arrived = lax.all_to_all(planes, "slab", split_axis=5, concat_axis=3, tiled=True).astype(
-        jnp.float32
-    )
-    depth_real = contract("wz,fczxy->fcxyw", depth_cos, arrived[0]) - contract(
-        "wz,fczxy->fcxyw", depth_sin, arrived[1]
-    )
-    depth_other = contract("wz,fczxy->fcxyw", depth_cos, arrived[1]) + contract(
-        "wz,fczxy->fcxyw", depth_sin, arrived[0]
-    )
-    sens_real = sens[0][None]
-    sens_other = sens[1][None]
-    combined_real = jnp.sum(sens_real * depth_real + sens_other * depth_other, axis=1)
-    combined_other = jnp.sum(sens_real * depth_other - sens_other * depth_real, axis=1)
-    matrix = jnp.stack([combined_real, combined_other], axis=1).transpose(0, 3, 1, 2, 4)
-    matrix = jnp.pad(matrix, ((0, 0), (0, 6), (0, 0), (0, 0), (0, 32))).reshape(2, 512, 128)
-    projected = merge(matrix, False).reshape(2, 32, 2, XW, 128)
+    projected = merge(front(kspace, sens), True).reshape(2, 32, 2, XW, 128)
     projected = projected[:, :26, :, :, :NZ].astype(jnp.float32)
     return projected.transpose(0, 2, 3, 1, 4)
 

time: 147 us -> 73 us (0.50)
  local copies, waits for them, and re-layouts: 60.8 us -> 3.19 us
  matrix products: 22.3 us -> 0 us
  Pallas kernels: 48.4 us -> 68.8 us
  waiting for transfers between devices: 8.69 us -> 0 us
  starting transfers between devices: 4.38 us -> 0 us
    squeeze x4 -> x0, local copies, waits for them, and re-layouts: 30 us -> none  [the longest x1 13.8 us: local(): spectrum[1]]
    dot_general x12 -> x0, matrix products: 22.3 us -> none  [contract(): jnp.einsum(pattern, matrix_table, operand, precision=lax.Precision.HIGHEST)]
    pallas_call x0 -> x1, Pallas kernels: none -> 19.1 us  [front(): pl.pallas_call(front_kernel, out_shape=jax.ShapeDtypeStruct((2, 512, 128)...]
    all_to_all x1 -> x0, waiting for transfers between devices: 8.69 us -> none  [local(): lax.all_to_all(planes, 'slab', split_axis=5, concat_axis=3, tiled=True)]
    unnamed x13 -> x6, local copies, waits for them, and re-layouts: 10.9 us -> 3.19 us
    slice x2 -> x0, local copies, waits for them, and re-layouts: 6.7 us -> none  [the longest x1 5.46 us: local(): spectrum[0]]
    another operation x1 -> x0, local copies, waits for them, and re-layouts: 5.79 us -> none  [local(): planes = jnp.stack([down_real, down_other]).astype(jnp.bfloat16)]
    all_to_all x1 -> x0, local copies, waits for them, and re-layouts: 4.38 us -> none  [local(): lax.all_to_all(planes, 'slab', split_axis=5, concat_axis=3, tiled=True)]
  transfers between devices with their start and end apart: 1 -> 0, of which waited for: 1 -> 0; matrix products, arithmetic and copies ran while one was open for 2% -> 0% of each run, Pallas kernels for 0% -> 0%
where the time goes in v3:
time: 73 us; the launch traced here: 72.8 us
  Pallas kernels  68.8 us (94%)
  local copies, waits for them, and re-layouts  3.19 us (4%)
  other arithmetic  0.79 us (1%)
    pallas_call x1, Pallas kernels, merge(): pl.pallas_call(lambda *refs: merge_kernel(flip, *refs), out_shape=jax.Sha...  49.7 us
    pallas_call x1, Pallas kernels, front(): pl.pallas_call(front_kernel, out_shape=jax.ShapeDtypeStruct((2, 512, 128)...  19.1 us
    unnamed x6, local copies, waits for them, and re-layouts  3.19 us

profile of v3, /device:TPU:0, one launch (start us, length us, event | category | flops | bytes accessed | tf_op | source)
XLA Modules:
  0.0 72.8 jit_solution(6530206716544236877)
XLA Ops:
  0.0 0.0 copy-start
  0.0 1.2 %copy-done = f32[2,4,8,26,96]{4,2,3,1,0:T(8,128)S(1)} copy-done((f32[2,4,8,26,96]{4,2,3,1,0:T(8,128)S(1)}, f32[2,4,8,26,96]{4,2,3,1,0:T(8,128)}, u32[]{:S(2)}) %copy-start) | copy-done | bytes 639000
  1.2 0.0 copy-start.1
  1.2 1.1 %copy-done.1 = bf16[256,1536]{1,0:T(8,128)(2,1)S(1)} copy-done((bf16[256,1536]{1,0:T(8,128)(2,1)S(1)}, bf16[256,1536]{1,0:T(8,128)(2,1)}, u32[]{:S(2)}) %copy-start.1) | copy-done | bytes 786456
  2.3 0.0 copy-start.2
  2.3 0.9 %copy-done.2 = bf16[256,256]{1,0:T(8,128)(2,1)S(1)} copy-done((bf16[256,256]{1,0:T(8,128)(2,1)S(1)}, bf16[256,256]{1,0:T(8,128)(2,1)}, u32[]{:S(2)}) %copy-start.2) | copy-done | bytes 131096
  3.2 19.1 %front.1.refs_0_ = f32[2,512,128]{2,1,0:T(8,128)S(1)} custom-call(bf16[2,192,9984]{2,1,0:T(8,128)(2,1)} %bitcast.9, f32[2,4,208,96]{3,2,1,0:T(8,128)S(1)} %bitcast.8, bf16[256,1536]{1,0:T(8,128)(2,1)S(1)} %copy-done.1, bf16[256,256]{1,0:T(8,128)(2,1)S(1)} %copy-done.2, bf16[2,4,320,1024]{3,2,1,0:T(8,128)(2,1)} %constant.8.clone.depth_ref), custom_call_target="tpu_custom_call" | custom-call | tf_op jit(solution)/shard_map/front/pallas_call | solution.py:374
  22.3 49.7 %merge.1 = bf16[2,512,128]{2,1,0:T(8,128)(2,1)S(1)} custom-call(f32[2,512,128]{2,1,0:T(8,128)S(1)} %front.1.refs_0_), custom_call_target="tpu_custom_call" | custom-call | tf_op jit(solution)/shard_map/merge/pallas_call | solution.py:180
  72.0 0.8 %convert_bitcast_fusion = f32[2,2,8,26,96]{4,2,3,1,0:T(8,128)} fusion(bf16[2,32,2,8,128]{4,3,2,1,0:T(8,128)(2,1)S(1)} %bitcast.7), kind=kLoop, calls=%fused_computation | loop fusion | flops 79872 | bytes 532480 | tf_op jit(solution)/shard_map/transpose | solution.py:407
Async XLA Ops:
  0.0 1.2 %copy-start = (f32[2,4,8,26,96]{4,2,3,1,0:T(8,128)S(1)}, f32[2,4,8,26,96]{4,2,3,1,0:T(8,128)}, u32[]{:S(2)}) copy-start(f32[2,4,8,26,96]{4,2,3,1,0:T(8,128)} %param.6) | copy-start | bytes 1916932
  1.2 1.1 %copy-start.1 = (bf16[256,1536]{1,0:T(8,128)(2,1)S(1)}, bf16[256,1536]{1,0:T(8,128)(2,1)}, u32[]{:S(2)}) copy-start(bf16[256,1536]{1,0:T(8,128)(2,1)} %constant.6.clone.across_ref) | copy-start | bytes 2359300
  2.3 0.9 %copy-start.2 = (bf16[256,256]{1,0:T(8,128)(2,1)S(1)}, bf16[256,256]{1,0:T(8,128)(2,1)}, u32[]{:S(2)}) copy-start(bf16[256,256]{1,0:T(8,128)(2,1)} %constant.7.clone.down_ref) | copy-start | bytes 393220

commit v4 on v3

v4 whole, which is shorter than its diff:
```python
import jax
import jax.numpy as jnp
import ml_dtypes
import numpy as np
from jax import lax
from jax.experimental import pallas as pl
from jax.experimental.pallas import tpu as pltpu
from jax.sharding import PartitionSpec as P

NX = 96
NY = 104
NZ = 96
RANK = 32
ITERS = 4
XW = 8
FRAMES = 64
ROWS = NY // 4
PANEL = 16


def matmul(left, right):
    return jnp.dot(
        left, right, precision=lax.Precision.HIGHEST, preferred_element_type=jnp.float32
    )


def dot_t(left, right):
    return lax.dot_general(
        left,
        right,
        (((1,), (1,)), ((), ())),
        precision=lax.Precision.HIGHEST,
        preferred_element_type=jnp.float32,
    )


def wait_bytes(ref, sem):
    pltpu.make_async_copy(ref, ref, sem).wait()


def eliminate(tables):
    tables = list(tables)
    row = lax.broadcasted_iota(jnp.int32, (RANK, 128), 0)
    lane = lax.broadcasted_iota(jnp.int32, (RANK, 128), 1)
    for k in range(0, RANK, PANEL):
        columns = [
            jnp.broadcast_to(tables[0][:, k + m : k + m + 1], (RANK, 128)) for m in range(PANEL)
        ]
        rows = [[table[k + m : k + m + 1, :] for m in range(PANEL)] for table in tables]
        for m in range(PANEL):
            inverse = 1.0 / columns[m][k + m : k + m + 1, :]
            factor = jnp.where(row > k + m, columns[m] * inverse, 0.0)
            for n in range(m + 1, PANEL):
                columns[n] = columns[n] - factor * columns[n][k + m : k + m + 1, :]
                for held in rows:
                    held[n] = held[n] - factor[k + n : k + n + 1, :] * held[m]
            for i, held in enumerate(rows):
                tables[i] = tables[i] - factor * held[m]
    diagonal = jnp.sum(jnp.where(lane == row, tables[0], 0.0), axis=1, keepdims=True)
    scale = lax.rsqrt(diagonal)
    return [table * scale for table in tables]


def root_coefficients(gram):
    pad = jnp.zeros((RANK, 32), jnp.float32)
    image = gram[:RANK] + gram[RANK:]
    inner = image[:, :RANK] + image[:, RANK:]
    for sweep in range(ITERS):
        (table,) = eliminate([jnp.concatenate([inner, image, pad], axis=1)])
        weights = table[:, RANK : RANK + FRAMES]
        image = matmul(weights, gram)
        inner = dot_t(image, weights)
    table, extra = eliminate(
        [
            jnp.concatenate([inner, image, pad], axis=1),
            jnp.concatenate([weights, pad, pad], axis=1),
        ]
    )
    return table[:, RANK : RANK + FRAMES], extra[:, :FRAMES]


def split_bf16(table):
    high = table.astype(ml_dtypes.bfloat16)
    low = (table - high.astype(np.float64)).astype(ml_dtypes.bfloat16)
    return high, low


def across_table():
    x = np.arange(XW) + (NX - XW) // 2
    angle = 2.0 * np.pi * (x[:, None] * np.arange(NX)[None, :] % NX) / NX
    cos, sin = np.cos(angle) / np.sqrt(NX), np.sin(angle) / np.sqrt(NX)
    table = np.zeros((XW, 2, 8, NX, 2, 8))
    for r in range(8):
        table[:, 0, r, :, 0, r] = cos
        table[:, 0, r, :, 1, r] = -sin
        table[:, 1, r, :, 0, r] = sin
        table[:, 1, r, :, 1, r] = cos
    return np.concatenate(split_bf16(table.reshape(XW * 16, NX * 16)), axis=0)


def down_table():
    angle = 2.0 * np.pi * (np.arange(NY)[:, None] * np.arange(NY)[None, :] % NY) / NY
    table = np.zeros((4, 32, 2, 128))
    table[:, :26, 0, :NY] = np.cos(angle).reshape(4, 26, NY) / np.sqrt(NY)
    table[:, :26, 1, :NY] = np.sin(angle).reshape(4, 26, NY) / np.sqrt(NY)
    return np.concatenate(split_bf16(table.reshape(128, 256)), axis=0)


def depth_table():
    angle = 2.0 * np.pi * (np.arange(NZ)[:, None] * np.arange(NZ)[None, :] % NZ) / NZ
    cos = (np.cos(angle) / np.sqrt(NZ)).reshape(4, 24, NZ)
    sin = (np.sin(angle) / np.sqrt(NZ)).reshape(4, 24, NZ)
    table = np.zeros((4, 2, 4, 24, 4, 2, 128))
    for c in range(4):
        table[:, 0, c, :, c, 0, :NZ] = cos
        table[:, 1, c, :, c, 0, :NZ] = -sin
        table[:, 0, c, :, c, 1, :NZ] = sin
        table[:, 1, c, :, c, 1, :NZ] = cos
    full = np.zeros((4, 320, 1024))
    full[:, 64:256] = table.reshape(4, 192, 1024)
    return np.stack(split_bf16(full))


def kernel(
    k_ref, sens_ref, across_ref, down_ref, depth_ref, out_ref,
    data, spec_hi, spec_lo, sent, got, acc, sens, across_tab, down_tab, depth,
    frames, recv, whole, outf, outb, gyz, gx, data_sems, table_sems, sems,
):
    me = lax.axis_index("tm")
    slab = lax.axis_index("slab")
    x_lo = me % 2
    mirror = me + 1 - 2 * x_lo
    x_pos = slab * 2 + x_lo
    yz_pos = me // 2

    def tm_peer(k):
        return (lax.rem(me + k, 32), slab)

    def x_peer(k):
        other = lax.rem(x_pos + k, 8)
        return (me - x_lo + other % 2, other // 2)

    def yz_peer(k):
        return (lax.rem(yz_pos + k, 16) * 2 + x_lo, slab)

    def fetch(g):
        rows = pl.ds(pl.multiple_of(g * 16, 16), 16)
        return pltpu.make_async_copy(k_ref.at[:, rows, :], data.at[:, rows, :], data_sems.at[g])

    def begin(g, c):
        fetch(g).start()
        return c

    across_copy = pltpu.make_async_copy(across_ref, across_tab, table_sems.at[0])
    down_copy = pltpu.make_async_copy(down_ref, down_tab, table_sems.at[1])
    depth_copy = pltpu.make_async_copy(depth_ref, depth, table_sems.at[2])
    sens_copy = pltpu.make_async_copy(sens_ref, sens, table_sems.at[3])
    fetch(0).start()
    across_copy.start()
    lax.fori_loop(1, 6, begin, 0)
    down_copy.start()
    lax.fori_loop(6, 12, begin, 0)
    depth_copy.start()
    sens_copy.start()

    barrier = pltpu.get_barrier_semaphore()

    def greet(peer):
        pl.semaphore_signal(barrier, inc=1, device_id=peer, device_id_type=pl.DeviceIdType.MESH)

    lax.fori_loop(1, 32, lambda k, c: (greet(tm_peer(k)), c)[1], 0)
    lax.fori_loop(1, 8, lambda k, c: (greet(x_peer(k)), c)[1], 0)
    frames[...] = jnp.zeros_like(frames)

    def send(src, dst, sem_at, peer):
        pltpu.make_async_remote_copy(
            src_ref=src,
            dst_ref=dst,
            send_sem=sems.at[sem_at],
            recv_sem=sems.at[sem_at + 1],
            device_id=peer,
            device_id_type=pl.DeviceIdType.MESH,
        ).start()

    def across(g, c):
        fetch(g).wait()
        rows = pl.ds(pl.multiple_of(g * 16, 16), 16)
        place = pl.multiple_of(lax.rem(g, 6) * 16, 16)
        total = jnp.zeros((256, 256), jnp.float32)
        lane = lax.broadcasted_iota(jnp.int32, (16, 128), 1)
        for t in range(6):
            lo, hi = t * 1664, (t + 1) * 1664
            real = data[0, rows, lo:hi].astype(jnp.float32)
            other = data[1, rows, lo:hi].astype(jnp.float32)
            parts = []
            for h in range(2):
                both = jnp.concatenate(
                    [real[h * 8 : h * 8 + 8], other[h * 8 : h * 8 + 8]], axis=0
                ).astype(jnp.bfloat16)
                pieces = []
                for a in range(16):
                    tile, off = divmod(a * 104, 128)
                    piece = both[:, tile * 128 : tile * 128 + 128]
                    if off > 24:
                        piece = jnp.where(lane >= off, piece, both[:, tile * 128 + 128 : tile * 128 + 256])
                    if off:
                        piece = pltpu.roll(piece, 128 - off, axis=1)
                    pieces.append(piece)
                parts.append(jnp.concatenate(pieces, axis=0))
            total = total + jnp.dot(
                across_tab[:, t * 256 : (t + 1) * 256],
                jnp.concatenate(parts, axis=1),
                preferred_element_type=jnp.float32,
            )
        image = total[:128] + total[128:]
        for j in range(XW):
            real = jnp.concatenate([image[j * 16 : j * 16 + 8, h * 128 : h * 128 + 128] for h in range(2)], axis=0)
            other = jnp.concatenate([image[j * 16 + 8 : j * 16 + 16, h * 128 : h * 128 + 128] for h in range(2)], axis=0)
            for part, pair in ((0, (real, -other)), (1, (other, real))):
                value = jnp.concatenate(pair, axis=1)
                high = value.astype(jnp.bfloat16)
                low = (value - high.astype(jnp.float32)).astype(jnp.bfloat16)
                at = pl.ds(place + ((j % 2) * 192 + part * 96), 16)
                spec_hi[j // 2, at, :] = high
                spec_lo[j // 2, at, :] = low
        return c

    def down(f):
        for jp in range(4):
            dims = (((1,), (1,)), ((), ()))
            first = lax.dot_general(down_tab[...], spec_hi[jp], dims, preferred_element_type=jnp.float32)
            second = lax.dot_general(down_tab[:128, :], spec_lo[jp], dims, preferred_element_type=jnp.float32)
            planes = (first[:128] + first[128:] + second).astype(jnp.bfloat16)
            for s in range(4):
                sent[f, s, jp * 32 : jp * 32 + 32, :] = planes[s * 32 : s * 32 + 32]

    across_copy.wait()
    for f in range(2):
        lax.fori_loop(6 * f, 6 * f + 6, across, 0)
        if f == 0:
            down_copy.wait()
        down(f)
        if f == 0:
            pl.semaphore_wait(barrier, 38)
        for s in range(4):
            send(sent.at[f, s], got.at[f, slab], 2 * f, (mirror, s))
    depth_copy.wait()
    sens_copy.wait()
    mine = pl.multiple_of(me * 16, 16)
    for f in range(2):
        wait_bytes(got.at[f], sems.at[2 * f + 1])
        for j2 in range(2):
            total = None
            for q in range(4):
                window = got[f, q, :, j2 * 128 : j2 * 128 + 256]
                for h in range(2):
                    term = jnp.dot(
                        window,
                        depth[h, q, 64 - 64 * j2 : 320 - 64 * j2, :],
                        preferred_element_type=jnp.float32,
                    )
                    total = term if total is None else total + term
            acc[...] = total
            for jp in range(4):
                j = jp * 2 + j2
                real = other = None
                for coil in range(4):
                    wave_real = acc[jp * 32 : jp * 32 + 26, coil * 256 : coil * 256 + 96]
                    wave_other = acc[jp * 32 : jp * 32 + 26, coil * 256 + 128 : coil * 256 + 224]
                    sens_real = sens[0, coil, pl.ds(j, 26, stride=8), :]
                    sens_other = sens[1, coil, pl.ds(j, 26, stride=8), :]
                    term_real = sens_real * wave_real + sens_other * wave_other
                    term_other = sens_real * wave_other - sens_other * wave_real
                    real = term_real if real is None else real + term_real
                    other = term_other if other is None else other + term_other
                pad = ((0, 0), (0, 32))
                frames[f, pl.ds(j, 26, stride=16), :] = jnp.pad(real, pad)
                frames[f, pl.ds(j + 8, 26, stride=16), :] = jnp.pad(other, pad)

        def scatter(k, c, f=f):
            peer = tm_peer(k)

            @pl.when(peer[0] < ROWS)
            def _():
                first = pl.multiple_of(peer[0] * 16, 16)
                send(frames.at[f, pl.ds(first, 16), :], recv.at[2 * mirror + f], 4, peer)

            return c

        lax.fori_loop(1, 32, scatter, 0)

    for f in range(2):
        wait_bytes(sent.at[f], sems.at[2 * f])

    @pl.when(me < ROWS)
    def _():
        for f in range(2):
            recv[2 * mirror + f] = frames[f, pl.ds(mine, 16), :]
        wait_bytes(frames.at[:, pl.ds(0, (ROWS - 1) * 16), :], sems.at[4])
        wait_bytes(recv.at[pl.ds(0, 62)], sems.at[5])
        flat = recv.reshape(FRAMES * 16, 128)
        for i in range(16):
            whole[:, i * 128 : (i + 1) * 128] = flat[pl.ds(i, FRAMES, stride=16), :]

    @pl.when(me >= ROWS)
    def _():
        wait_bytes(frames.at[:, pl.ds(0, ROWS * 16), :], sems.at[4])
        whole[...] = jnp.zeros_like(whole)

    gram = dot_t(whole[...], whole[...])
    packed = jnp.concatenate([gram[:32], gram[32:]], axis=1)

    def all_sum(value, buf, pos, count, peer_of, sem_at):
        buf[pl.ds(pos, 1)] = value[None]

        def tell(k, c):
            send(buf.at[pl.ds(pos, 1)], buf.at[pl.ds(pos, 1)], sem_at, peer_of(k))
            return c

        lax.fori_loop(1, count, tell, 0)
        wait_bytes(buf.at[pl.ds(0, count - 1)], sems.at[sem_at])
        wait_bytes(buf.at[pl.ds(0, count - 1)], sems.at[sem_at + 1])
        total = buf[0]
        for k in range(1, count):
            total = total + buf[k]
        return total

    packed = all_sum(packed, gyz, yz_pos, 16, yz_peer, 6)
    packed = all_sum(packed, gx, x_pos, 8, x_peer, 8)
    gram = jnp.concatenate([packed[:, :64], packed[:, 64:]], axis=0)
    image, coeff = root_coefficients(gram)
    mixing = lax.dot_general(
        image,
        coeff,
        (((0,), (0,)), ((), ())),
        precision=lax.Precision.HIGHEST,
        preferred_element_type=jnp.float32,
    )

    @pl.when(me < ROWS)
    def _():
        for i in range(16):
            outf[pl.ds(i, FRAMES, stride=16), :] = matmul(mixing, whole[:, i * 128 : (i + 1) * 128])
        outb[...] = outf[...].reshape(FRAMES, 16, 128).astype(jnp.bfloat16)

        def give(k, c):
            peer = tm_peer(k)
            send(outb.at[pl.ds(2 * peer[0], 2)], out_ref.at[:, pl.ds(mine, 16), :], 10, peer)
            return c

        lax.fori_loop(1, 32, give, 0)
        out_ref[:, pl.ds(mine, 16), :] = outb[pl.ds(2 * me, 2)]
        wait_bytes(outb.at[pl.ds(0, 62)], sems.at[10])
        wait_bytes(out_ref.at[:, pl.ds(0, (ROWS - 1) * 16), :], sems.at[11])

    @pl.when(me >= ROWS)
    def _():
        wait_bytes(out_ref, sems.at[11])


def local(kspace, sens):
    hbm = pl.BlockSpec(memory_space=pltpu.HBM)
    projected = pl.pallas_call(
        kernel,
        out_shape=jax.ShapeDtypeStruct((2, ROWS * 16, 128), jnp.bfloat16),
        in_specs=[hbm] * 5,
        out_specs=pl.BlockSpec(memory_space=pltpu.VMEM),
        scratch_shapes=[
            pltpu.VMEM((2, 192, 9984), jnp.bfloat16),
            pltpu.VMEM((4, 384, 256), jnp.bfloat16),
            pltpu.VMEM((4, 384, 256), jnp.bfloat16),
            pltpu.VMEM((2, 4, 128, 384), jnp.bfloat16),
            pltpu.VMEM((2, 4, 128, 384), jnp.bfloat16),
            pltpu.VMEM((128, 1024), jnp.float32),
            pltpu.VMEM((2, 4, 208, NZ), jnp.float32),
            pltpu.VMEM((256, 1536), jnp.bfloat16),
            pltpu.VMEM((256, 256), jnp.bfloat16),
            pltpu.VMEM((2, 4, 320, 1024), jnp.bfloat16),
            pltpu.VMEM((2, 512, 128), jnp.float32),
            pltpu.VMEM((FRAMES, 16, 128), jnp.float32),
            pltpu.VMEM((FRAMES, 2048), jnp.float32),
            pltpu.VMEM((FRAMES * 16, 128), jnp.float32),
            pltpu.VMEM((FRAMES, 16, 128), jnp.bfloat16),
            pltpu.VMEM((16, 32, 128), jnp.float32),
            pltpu.VMEM((8, 32, 128), jnp.float32),
            pltpu.SemaphoreType.DMA((12,)),
            pltpu.SemaphoreType.DMA((4,)),
            pltpu.SemaphoreType.DMA((12,)),
        ],
        compiler_params=pltpu.CompilerParams(
            collective_id=0, has_side_effects=True, vmem_limit_bytes=56 * 1024 * 1024
        ),
        name="frames_to_projection",
    )(
        kspace.reshape(2, 192, NX * NY),
        sens.transpose(0, 1, 3, 2, 4).reshape(2, 4, 208, NZ),
        across_table(),
        down_table(),
        depth_table(),
    )
    projected = projected.reshape(2, ROWS, 2, XW, 128)[..., :NZ].astype(jnp.float32)
    return projected.transpose(0, 2, 3, 1, 4)


def solution(mesh):
    in_specs = (P(None, "tm", None, "slab", None), P(None, None, None, "slab", None))
    out_specs = P("tm", None, None, "slab", None)
    return jax.shard_map(local, mesh=mesh, in_specs=in_specs, out_specs=out_specs, check_vma=False)
```

time: 73 us -> 53.3 us (0.73)
  Pallas kernels: 68.8 us -> 50.7 us
  local copies, waits for them, and re-layouts: 3.19 us -> 0 us
  other arithmetic: 0.79 us -> 1.72 us
    pallas_call x2 -> x1, Pallas kernels: 68.8 us -> 50.7 us  [local(): pl.pallas_call(kernel, out_shape=jax.ShapeDtypeStruct((2, ROWS * 16, 128)...]
    unnamed x6 -> x0, local copies, waits for them, and re-layouts: 3.19 us -> none
    transpose x1, other arithmetic: 0.79 us -> 1.72 us  [local(): return projected.transpose(0, 2, 3, 1, 4)]
where the time goes in v4:
time: 53.3 us; the launch traced here: 52.4 us
  Pallas kernels  50.7 us (95%)
  other arithmetic  1.72 us (3%)
    pallas_call x1, Pallas kernels, local(): pl.pallas_call(kernel, out_shape=jax.ShapeDtypeStruct((2, ROWS * 16, 128)...  50.7 us
    transpose x1, other arithmetic, local(): return projected.transpose(0, 2, 3, 1, 4)  1.72 us

profile of v4, /device:TPU:0, one launch (start us, length us, event | category | flops | bytes accessed | tf_op | source)
XLA Modules:
  0.0 52.4 jit_solution(810356297525026890)
XLA Ops:
  0.0 50.7 %frames_to_projection.1 = bf16[2,416,128]{2,1,0:T(8,128)(2,1)} custom-call(bf16[2,192,9984]{2,1,0:T(8,128)(2,1)} %bitcast.7, f32[2,4,208,96]{3,2,1,0:T(8,128)} %bitcast.8, bf16[256,1536]{1,0:T(8,128)(2,1)} %constant.6.clone.across_ref, bf16[256,256]{1,0:T(8,128)(2,1)} %constant.7.clone.down_ref, bf16[2,4,320,1024]{3,2,1,0:T(8,128)(2,1)} %constant.8.clone.depth_ref), custom_call_target="tpu_custom_call" | custom-call | tf_op jit(solution)/shard_map/frames_to_projection/pallas_call | solution.py:363
  50.7 1.7 %convert_bitcast_fusion = f32[2,2,8,26,96]{4,2,3,1,0:T(8,128)} fusion(bf16[2,26,2,8,128]{4,3,2,1,0:T(8,128)(2,1)} %bitcast.9), kind=kLoop, calls=%fused_computation | loop fusion | flops 79872 | bytes 532480 | tf_op jit(solution)/shard_map/transpose | solution.py:402

commit v5 on v4

--- a/solution.py
+++ b/solution.py
@@ -110,28 +110,28 @@
     angle = 2.0 * np.pi * (np.arange(NZ)[:, None] * np.arange(NZ)[None, :] % NZ) / NZ
     cos = (np.cos(angle) / np.sqrt(NZ)).reshape(4, 24, NZ)
     sin = (np.sin(angle) / np.sqrt(NZ)).reshape(4, 24, NZ)
-    table = np.zeros((4, 2, 4, 24, 4, 2, 128))
-    for c in range(4):
+    table = np.zeros((4, 2, 2, 24, 2, 2, 128))
+    for c in range(2):
         table[:, 0, c, :, c, 0, :NZ] = cos
         table[:, 1, c, :, c, 0, :NZ] = -sin
         table[:, 0, c, :, c, 1, :NZ] = sin
         table[:, 1, c, :, c, 1, :NZ] = cos
-    full = np.zeros((4, 320, 1024))
-    full[:, 64:256] = table.reshape(4, 192, 1024)
-    return np.stack(split_bf16(full))
+    full = np.zeros((4, 128, 512))
+    full[:, :96] = table.reshape(4, 96, 512)
+    return np.stack(split_bf16(full.reshape(512, 512)))
 
 
 def kernel(
-    k_ref, sens_ref, across_ref, down_ref, depth_ref, out_ref,
-    data, spec_hi, spec_lo, sent, got, acc, sens, across_tab, down_tab, depth,
-    frames, recv, whole, outf, outb, gyz, gx, data_sems, table_sems, sems,
+    k_ref, sens_ref, plane_ref, depth_ref, out_ref,
+    data, spec_hi, spec_lo, sent, got, acc, sens, plane_tab, depth,
+    frames, recv, whole, outf, outb, g_row, g_plane, data_sems, table_sems, sems,
 ):
     me = lax.axis_index("tm")
     slab = lax.axis_index("slab")
     x_lo = me % 2
-    mirror = me + 1 - 2 * x_lo
     x_pos = slab * 2 + x_lo
     yz_pos = me // 2
+    far = lax.rem(slab + 2, 4)
 
     def tm_peer(k):
         return (lax.rem(me + k, 32), slab)
@@ -151,15 +151,12 @@
         fetch(g).start()
         return c
 
-    across_copy = pltpu.make_async_copy(across_ref, across_tab, table_sems.at[0])
-    down_copy = pltpu.make_async_copy(down_ref, down_tab, table_sems.at[1])
-    depth_copy = pltpu.make_async_copy(depth_ref, depth, table_sems.at[2])
-    sens_copy = pltpu.make_async_copy(sens_ref, sens, table_sems.at[3])
+    plane_copy = pltpu.make_async_copy(plane_ref, plane_tab, table_sems.at[0])
+    depth_copy = pltpu.make_async_copy(depth_ref, depth, table_sems.at[1])
+    sens_copy = pltpu.make_async_copy(sens_ref, sens, table_sems.at[2])
     fetch(0).start()
-    across_copy.start()
-    lax.fori_loop(1, 6, begin, 0)
-    down_copy.start()
-    lax.fori_loop(6, 12, begin, 0)
+    plane_copy.start()
+    lax.fori_loop(1, 12, begin, 0)
     depth_copy.start()
     sens_copy.start()
 
@@ -185,7 +182,7 @@
     def across(g, c):
         fetch(g).wait()
         rows = pl.ds(pl.multiple_of(g * 16, 16), 16)
-        place = pl.multiple_of(lax.rem(g, 6) * 16, 16)
+        place = pl.multiple_of(lax.rem(g, 3) * 16, 16)
         total = jnp.zeros((256, 256), jnp.float32)
         lane = lax.broadcasted_iota(jnp.int32, (16, 128), 1)
         for t in range(6):
@@ -208,7 +205,7 @@
                     pieces.append(piece)
                 parts.append(jnp.concatenate(pieces, axis=0))
             total = total + jnp.dot(
-                across_tab[:, t * 256 : (t + 1) * 256],
+                plane_tab[:, t * 256 : (t + 1) * 256],
                 jnp.concatenate(parts, axis=1),
                 preferred_element_type=jnp.float32,
             )
@@ -220,62 +217,72 @@
                 value = jnp.concatenate(pair, axis=1)
                 high = value.astype(jnp.bfloat16)
                 low = (value - high.astype(jnp.float32)).astype(jnp.bfloat16)
-                at = pl.ds(place + ((j % 2) * 192 + part * 96), 16)
-                spec_hi[j // 2, at, :] = high
-                spec_lo[j // 2, at, :] = low
+                at = pl.ds(place + ((j % 4) * 96 + part * 48), 16)
+                spec_hi[j // 4, at, :] = high
+                spec_lo[j // 4, at, :] = low
         return c
 
-    def down(f):
-        for jp in range(4):
+    def down(chunk):
+        for jq in range(2):
             dims = (((1,), (1,)), ((), ()))
-            first = lax.dot_general(down_tab[...], spec_hi[jp], dims, preferred_element_type=jnp.float32)
-            second = lax.dot_general(down_tab[:128, :], spec_lo[jp], dims, preferred_element_type=jnp.float32)
+            first = lax.dot_general(plane_tab[:, 1536:], spec_hi[jq], dims, preferred_element_type=jnp.float32)
+            second = lax.dot_general(plane_tab[:128, 1536:], spec_lo[jq], dims, preferred_element_type=jnp.float32)
             planes = (first[:128] + first[128:] + second).astype(jnp.bfloat16)
             for s in range(4):
-                sent[f, s, jp * 32 : jp * 32 + 32, :] = planes[s * 32 : s * 32 + 32]
-
-    across_copy.wait()
-    for f in range(2):
-        lax.fori_loop(6 * f, 6 * f + 6, across, 0)
-        if f == 0:
-            down_copy.wait()
-        down(f)
-        if f == 0:
+                sent[chunk, s, jq * 32 : jq * 32 + 32, :] = planes[s * 32 : s * 32 + 32]
+
+    plane_copy.wait()
+    for chunk in range(4):
+        lax.fori_loop(3 * chunk, 3 * chunk + 3, across, 0)
+        down(chunk)
+        if chunk == 0:
             pl.semaphore_wait(barrier, 38)
-        for s in range(4):
-            send(sent.at[f, s], got.at[f, slab], 2 * f, (mirror, s))
+        for other in (far, far + 1 - 2 * (slab % 2), slab + 1 - 2 * (slab % 2)):
+            send(sent.at[chunk, other], got.at[chunk, slab], 2 * chunk, (me, other))
+        got[chunk, pl.ds(slab, 1)] = sent[chunk, pl.ds(slab, 1)]
     depth_copy.wait()
     sens_copy.wait()
     mine = pl.multiple_of(me * 16, 16)
-    for f in range(2):
-        wait_bytes(got.at[f], sems.at[2 * f + 1])
-        for j2 in range(2):
-            total = None
-            for q in range(4):
-                window = got[f, q, :, j2 * 128 : j2 * 128 + 256]
-                for h in range(2):
-                    term = jnp.dot(
-                        window,
-                        depth[h, q, 64 - 64 * j2 : 320 - 64 * j2, :],
-                        preferred_element_type=jnp.float32,
-                    )
-                    total = term if total is None else total + term
-            acc[...] = total
-            for jp in range(4):
-                j = jp * 2 + j2
+    for chunk in range(4):
+        f, pair = divmod(chunk, 2)
+        wait_bytes(got.at[chunk, pl.ds(0, 3)], sems.at[2 * chunk + 1])
+        lane = lax.broadcasted_iota(jnp.int32, (64, 128), 1)
+        blocks = []
+        for q in range(4):
+            third = [got[chunk, q, :, t * 128 : t * 128 + 128] for t in range(3)]
+            pieces = (
+                third[0],
+                pltpu.roll(jnp.where(lane >= 96, third[0], third[1]), 32, axis=1),
+                pltpu.roll(jnp.where(lane >= 64, third[1], third[2]), 64, axis=1),
+                pltpu.roll(third[2], 96, axis=1),
+            )
+            blocks.append(jnp.concatenate(pieces, axis=0))
+        gathered = jnp.concatenate(blocks, axis=1)
+        acc[...] = jnp.dot(gathered, depth[0], preferred_element_type=jnp.float32) + jnp.dot(
+            gathered, depth[1], preferred_element_type=jnp.float32
+        )
+        for jq in range(2):
+            for j4 in range(4):
+                j = jq * 4 + j4
                 real = other = None
-                for coil in range(4):
-                    wave_real = acc[jp * 32 : jp * 32 + 26, coil * 256 : coil * 256 + 96]
-                    wave_other = acc[jp * 32 : jp * 32 + 26, coil * 256 + 128 : coil * 256 + 224]
-                    sens_real = sens[0, coil, pl.ds(j, 26, stride=8), :]
-                    sens_other = sens[1, coil, pl.ds(j, 26, stride=8), :]
+                for c in range(2):
+                    rows = slice(j4 * 64 + jq * 32, j4 * 64 + jq * 32 + 26)
+                    wave_real = acc[rows, c * 256 : c * 256 + 96]
+                    wave_other = acc[rows, c * 256 + 128 : c * 256 + 224]
+                    sens_real = sens[0, pair * 2 + c, pl.ds(j, 26, stride=8), :]
+                    sens_other = sens[1, pair * 2 + c, pl.ds(j, 26, stride=8), :]
                     term_real = sens_real * wave_real + sens_other * wave_other
                     term_other = sens_real * wave_other - sens_other * wave_real
                     real = term_real if real is None else real + term_real
                     other = term_other if other is None else other + term_other
                 pad = ((0, 0), (0, 32))
-                frames[f, pl.ds(j, 26, stride=16), :] = jnp.pad(real, pad)
-                frames[f, pl.ds(j + 8, 26, stride=16), :] = jnp.pad(other, pad)
+                real, other = jnp.pad(real, pad), jnp.pad(other, pad)
+                at_real, at_other = pl.ds(j, 26, stride=16), pl.ds(j + 8, 26, stride=16)
+                if pair:
+                    real = real + frames[f, at_real, :]
+                    other = other + frames[f, at_other, :]
+                frames[f, at_real, :] = real
+                frames[f, at_other, :] = other
 
         def scatter(k, c, f=f):
             peer = tm_peer(k)
@@ -283,50 +290,71 @@
             @pl.when(peer[0] < ROWS)
             def _():
                 first = pl.multiple_of(peer[0] * 16, 16)
-                send(frames.at[f, pl.ds(first, 16), :], recv.at[2 * mirror + f], 4, peer)
+                send(frames.at[f, pl.ds(first, 16), :], recv.at[2 * me + f], 8, peer)
 
             return c
 
-        lax.fori_loop(1, 32, scatter, 0)
-
-    for f in range(2):
-        wait_bytes(sent.at[f], sems.at[2 * f])
+        if pair:
+            lax.fori_loop(1, 32, scatter, 0)
 
     @pl.when(me < ROWS)
     def _():
         for f in range(2):
-            recv[2 * mirror + f] = frames[f, pl.ds(mine, 16), :]
-        wait_bytes(frames.at[:, pl.ds(0, (ROWS - 1) * 16), :], sems.at[4])
-        wait_bytes(recv.at[pl.ds(0, 62)], sems.at[5])
+            recv[2 * me + f] = frames[f, pl.ds(mine, 16), :]
+        wait_bytes(recv.at[pl.ds(0, 62)], sems.at[9])
         flat = recv.reshape(FRAMES * 16, 128)
         for i in range(16):
-            whole[:, i * 128 : (i + 1) * 128] = flat[pl.ds(i, FRAMES, stride=16), :]
+            value = flat[pl.ds(i, FRAMES, stride=16), :]
+            high = value.astype(jnp.bfloat16)
+            whole[:FRAMES, i * 128 : (i + 1) * 128] = high
+            whole[FRAMES:, i * 128 : (i + 1) * 128] = (value - high.astype(jnp.float32)).astype(jnp.bfloat16)
 
     @pl.when(me >= ROWS)
     def _():
-        wait_bytes(frames.at[:, pl.ds(0, ROWS * 16), :], sems.at[4])
         whole[...] = jnp.zeros_like(whole)
 
-    gram = dot_t(whole[...], whole[...])
+    quarters = lax.dot_general(
+        whole[...], whole[...], (((1,), (1,)), ((), ())), preferred_element_type=jnp.float32
+    )
+    halves = quarters[:FRAMES] + quarters[FRAMES:]
+    gram = halves[:, :FRAMES] + halves[:, FRAMES:]
     packed = jnp.concatenate([gram[:32], gram[32:]], axis=1)
 
-    def all_sum(value, buf, pos, count, peer_of, sem_at):
-        buf[pl.ds(pos, 1)] = value[None]
-
-        def tell(k, c):
-            send(buf.at[pl.ds(pos, 1)], buf.at[pl.ds(pos, 1)], sem_at, peer_of(k))
+    def tell(slot, sem_at, count, peer_of):
+        def one(k, c):
+            send(slot, slot, sem_at, peer_of(k))
             return c
 
-        lax.fori_loop(1, count, tell, 0)
+        lax.fori_loop(1, count, one, 0)
+
+    def heard(buf, count, sem_at):
         wait_bytes(buf.at[pl.ds(0, count - 1)], sems.at[sem_at])
         wait_bytes(buf.at[pl.ds(0, count - 1)], sems.at[sem_at + 1])
+
+    def summed(buf, count):
         total = buf[0]
         for k in range(1, count):
             total = total + buf[k]
         return total
 
-    packed = all_sum(packed, gyz, yz_pos, 16, yz_peer, 6)
-    packed = all_sum(packed, gx, x_pos, 8, x_peer, 8)
+    g_plane[pl.ds(yz_pos, 1)] = packed[None]
+    tell(g_plane.at[pl.ds(yz_pos, 1)], 10, 16, yz_peer)
+    for chunk in range(4):
+        wait_bytes(sent.at[chunk, pl.ds(0, 3)], sems.at[2 * chunk])
+
+    @pl.when(me < ROWS)
+    def _():
+        wait_bytes(frames.at[:, pl.ds(0, (ROWS - 1) * 16), :], sems.at[8])
+
+    @pl.when(me >= ROWS)
+    def _():
+        wait_bytes(frames.at[:, pl.ds(0, ROWS * 16), :], sems.at[8])
+
+    heard(g_plane, 16, 10)
+    g_row[pl.ds(x_pos, 1)] = summed(g_plane, 16)[None]
+    tell(g_row.at[pl.ds(x_pos, 1)], 12, 8, x_peer)
+    heard(g_row, 8, 12)
+    packed = summed(g_row, 8)
     gram = jnp.concatenate([packed[:, :64], packed[:, 64:]], axis=0)
     image, coeff = root_coefficients(gram)
     mixing = lax.dot_general(
@@ -339,23 +367,31 @@
 
     @pl.when(me < ROWS)
     def _():
+        high = mixing.astype(jnp.bfloat16)
+        low = (mixing - high.astype(jnp.float32)).astype(jnp.bfloat16)
+        left = jnp.concatenate(
+            [jnp.concatenate([high, high], axis=1), jnp.concatenate([low, low], axis=1)], axis=0
+        )
         for i in range(16):
-            outf[pl.ds(i, FRAMES, stride=16), :] = matmul(mixing, whole[:, i * 128 : (i + 1) * 128])
+            both = jnp.dot(
+                left, whole[:, i * 128 : (i + 1) * 128], preferred_element_type=jnp.float32
+            )
+            outf[pl.ds(i, FRAMES, stride=16), :] = both[:FRAMES] + both[FRAMES:]
         outb[...] = outf[...].reshape(FRAMES, 16, 128).astype(jnp.bfloat16)
 
         def give(k, c):
             peer = tm_peer(k)
-            send(outb.at[pl.ds(2 * peer[0], 2)], out_ref.at[:, pl.ds(mine, 16), :], 10, peer)
+            send(outb.at[pl.ds(2 * peer[0], 2)], out_ref.at[:, pl.ds(mine, 16), :], 16, peer)
             return c
 
         lax.fori_loop(1, 32, give, 0)
         out_ref[:, pl.ds(mine, 16), :] = outb[pl.ds(2 * me, 2)]
-        wait_bytes(outb.at[pl.ds(0, 62)], sems.at[10])
-        wait_bytes(out_ref.at[:, pl.ds(0, (ROWS - 1) * 16), :], sems.at[11])
+        wait_bytes(outb.at[pl.ds(0, 62)], sems.at[16])
+        wait_bytes(out_ref.at[:, pl.ds(0, (ROWS - 1) * 16), :], sems.at[17])
 
     @pl.when(me >= ROWS)
     def _():
-        wait_bytes(out_ref, sems.at[11])
+        wait_bytes(out_ref, sems.at[17])
 
 
 def local(kspace, sens):
@@ -363,39 +399,37 @@
     projected = pl.pallas_call(
         kernel,
         out_shape=jax.ShapeDtypeStruct((2, ROWS * 16, 128), jnp.bfloat16),
-        in_specs=[hbm] * 5,
+        in_specs=[hbm] * 4,
         out_specs=pl.BlockSpec(memory_space=pltpu.VMEM),
         scratch_shapes=[
             pltpu.VMEM((2, 192, 9984), jnp.bfloat16),
-            pltpu.VMEM((4, 384, 256), jnp.bfloat16),
-            pltpu.VMEM((4, 384, 256), jnp.bfloat16),
-            pltpu.VMEM((2, 4, 128, 384), jnp.bfloat16),
-            pltpu.VMEM((2, 4, 128, 384), jnp.bfloat16),
-            pltpu.VMEM((128, 1024), jnp.float32),
+            pltpu.VMEM((2, 384, 256), jnp.bfloat16),
+            pltpu.VMEM((2, 384, 256), jnp.bfloat16),
+            pltpu.VMEM((4, 4, 64, 384), jnp.bfloat16),
+            pltpu.VMEM((4, 4, 64, 384), jnp.bfloat16),
+            pltpu.VMEM((256, 512), jnp.float32),
             pltpu.VMEM((2, 4, 208, NZ), jnp.float32),
-            pltpu.VMEM((256, 1536), jnp.bfloat16),
-            pltpu.VMEM((256, 256), jnp.bfloat16),
-            pltpu.VMEM((2, 4, 320, 1024), jnp.bfloat16),
+            pltpu.VMEM((256, 1792), jnp.bfloat16),
+            pltpu.VMEM((2, 512, 512), jnp.bfloat16),
             pltpu.VMEM((2, 512, 128), jnp.float32),
             pltpu.VMEM((FRAMES, 16, 128), jnp.float32),
-            pltpu.VMEM((FRAMES, 2048), jnp.float32),
+            pltpu.VMEM((2 * FRAMES, 2048), jnp.bfloat16),
             pltpu.VMEM((FRAMES * 16, 128), jnp.float32),
             pltpu.VMEM((FRAMES, 16, 128), jnp.bfloat16),
+            pltpu.VMEM((8, 32, 128), jnp.float32),
             pltpu.VMEM((16, 32, 128), jnp.float32),
-            pltpu.VMEM((8, 32, 128), jnp.float32),
             pltpu.SemaphoreType.DMA((12,)),
-            pltpu.SemaphoreType.DMA((4,)),
-            pltpu.SemaphoreType.DMA((12,)),
+            pltpu.SemaphoreType.DMA((3,)),
+            pltpu.SemaphoreType.DMA((18,)),
         ],
         compiler_params=pltpu.CompilerParams(
-            collective_id=0, has_side_effects=True, vmem_limit_bytes=56 * 1024 * 1024
+            collective_id=0, has_side_effects=True, vmem_limit_bytes=54784 * 1024
         ),
         name="frames_to_projection",
     )(
         kspace.reshape(2, 192, NX * NY),
         sens.transpose(0, 1, 3, 2, 4).reshape(2, 4, 208, NZ),
-        across_table(),
-        down_table(),
+        np.concatenate([across_table(), down_table()], axis=1),
         depth_table(),
     )
     projected = projected.reshape(2, ROWS, 2, XW, 128)[..., :NZ].astype(jnp.float32)

time: 53.3 us -> 49.5 us (0.929); the launches traced: 52.4 us -> 49.4 us
  Pallas kernels: 50.7 us -> 48.6 us
  other arithmetic: 1.72 us -> 0.79 us
    pallas_call x1, Pallas kernels: 50.7 us -> 48.6 us  [local(): pl.pallas_call(kernel, out_shape=jax.ShapeDtypeStruct((2, ROWS * 16, 128)...]
    transpose x1, other arithmetic: 1.72 us -> 0.79 us  [local(): return projected.transpose(0, 2, 3, 1, 4)]
where the time goes in v5:
time: 49.5 us; the launch traced here: 49.4 us
  Pallas kernels  48.6 us (98%)
  other arithmetic  0.79 us (2%)
    pallas_call x1, Pallas kernels, local(): pl.pallas_call(kernel, out_shape=jax.ShapeDtypeStruct((2, ROWS * 16, 128)...  48.6 us

profile of v5, /device:TPU:0, one launch (start us, length us, event | category | flops | bytes accessed | tf_op | source)
XLA Modules:
  0.0 49.4 jit_solution(1000938258813993078)
XLA Ops:
  0.0 48.6 %frames_to_projection.1 = bf16[2,416,128]{2,1,0:T(8,128)(2,1)S(1)} custom-call(bf16[2,192,9984]{2,1,0:T(8,128)(2,1)} %bitcast.8, f32[2,4,208,96]{3,2,1,0:T(8,128)} %bitcast.9, bf16[256,1792]{1,0:T(8,128)(2,1)} %constant.4.clone.plane_ref, bf16[2,512,512]{2,1,0:T(8,128)(2,1)} %constant.5.clone.depth_ref), custom_call_target="tpu_custom_call" | custom-call | tf_op jit(solution)/shard_map/frames_to_projection/pallas_call | solution.py:399
  48.6 0.8 %convert_bitcast_fusion = f32[2,2,8,26,96]{4,2,3,1,0:T(8,128)} fusion(bf16[2,26,2,8,128]{4,3,2,1,0:T(8,128)(2,1)S(1)} %bitcast.7), kind=kLoop, calls=%fused_computation | loop fusion | flops 79872 | bytes 532480 | tf_op jit(solution)/shard_map/transpose | solution.py:436

commit v6 on v5

--- a/solution.py
+++ b/solution.py
@@ -156,17 +156,18 @@
     sens_copy = pltpu.make_async_copy(sens_ref, sens, table_sems.at[2])
     fetch(0).start()
     plane_copy.start()
-    lax.fori_loop(1, 12, begin, 0)
+    lax.fori_loop(1, 3, begin, 0)
+    barrier = pltpu.get_barrier_semaphore()
+
+    def greet(peer):
+        pl.semaphore_signal(barrier, inc=1, device_id=peer, device_id_type=pl.DeviceIdType.MESH)
+
+    lax.fori_loop(1, 32, lambda k, c: (greet(tm_peer(k)), c)[1], 0)
+    lax.fori_loop(1, 8, lambda k, c: (greet(x_peer(k)), c)[1], 0)
+    lax.fori_loop(3, 12, begin, 0)
     depth_copy.start()
     sens_copy.start()
 
-    barrier = pltpu.get_barrier_semaphore()
-
-    def greet(peer):
-        pl.semaphore_signal(barrier, inc=1, device_id=peer, device_id_type=pl.DeviceIdType.MESH)
-
-    lax.fori_loop(1, 32, lambda k, c: (greet(tm_peer(k)), c)[1], 0)
-    lax.fori_loop(1, 8, lambda k, c: (greet(x_peer(k)), c)[1], 0)
     frames[...] = jnp.zeros_like(frames)
 
     def send(src, dst, sem_at, peer):
@@ -337,8 +338,8 @@
             total = total + buf[k]
         return total
 
-    g_plane[pl.ds(yz_pos, 1)] = packed[None]
-    tell(g_plane.at[pl.ds(yz_pos, 1)], 10, 16, yz_peer)
+    g_row[pl.ds(x_pos, 1)] = packed[None]
+    tell(g_row.at[pl.ds(x_pos, 1)], 12, 8, x_peer)
     for chunk in range(4):
         wait_bytes(sent.at[chunk, pl.ds(0, 3)], sems.at[2 * chunk])
 
@@ -350,11 +351,11 @@
     def _():
         wait_bytes(frames.at[:, pl.ds(0, ROWS * 16), :], sems.at[8])
 
+    heard(g_row, 8, 12)
+    g_plane[pl.ds(yz_pos, 1)] = summed(g_row, 8)[None]
+    tell(g_plane.at[pl.ds(yz_pos, 1)], 10, 16, yz_peer)
     heard(g_plane, 16, 10)
-    g_row[pl.ds(x_pos, 1)] = summed(g_plane, 16)[None]
-    tell(g_row.at[pl.ds(x_pos, 1)], 12, 8, x_peer)
-    heard(g_row, 8, 12)
-    packed = summed(g_row, 8)
+    packed = summed(g_plane, 16)
     gram = jnp.concatenate([packed[:, :64], packed[:, 64:]], axis=0)
     image, coeff = root_coefficients(gram)
     mixing = lax.dot_general(

time: 49.5 us -> 49.3 us (level)
  no operation moved by 1% of the time
where the time goes in v6:
time: 49.3 us; the launch traced here: 49.2 us
  Pallas kernels  48.4 us (98%)
  other arithmetic  0.79 us (2%)
    pallas_call x1, Pallas kernels, local(): pl.pallas_call(kernel, out_shape=jax.ShapeDtypeStruct((2, ROWS * 16, 128)...  48.4 us

profile of v6, /device:TPU:0, one launch (start us, length us, event | category | flops | bytes accessed | tf_op | source)
XLA Modules:
  0.0 49.2 jit_solution(17501886093447455859)
XLA Ops:
  0.0 48.4 %frames_to_projection.1 = bf16[2,416,128]{2,1,0:T(8,128)(2,1)S(1)} custom-call(bf16[2,192,9984]{2,1,0:T(8,128)(2,1)} %bitcast.8, f32[2,4,208,96]{3,2,1,0:T(8,128)} %bitcast.9, bf16[256,1792]{1,0:T(8,128)(2,1)} %constant.4.clone.plane_ref, bf16[2,512,512]{2,1,0:T(8,128)(2,1)} %constant.5.clone.depth_ref), custom_call_target="tpu_custom_call" | custom-call | tf_op jit(solution)/shard_map/frames_to_projection/pallas_call | solution.py:400
  48.4 0.8 %convert_bitcast_fusion = f32[2,2,8,26,96]{4,2,3,1,0:T(8,128)} fusion(bf16[2,26,2,8,128]{4,3,2,1,0:T(8,128)(2,1)S(1)} %bitcast.7), kind=kLoop, calls=%fused_computation | loop fusion | flops 79872 | bytes 532480 | tf_op jit(solution)/shard_map/transpose | solution.py:437
